TPU v7x, 32 devices: a whole 2x2x4 slice. The times are simulated.
32 devices in a mesh: ctx: 4 (over x, core), fsdp: 8 (over z, y).
Axes of the slice: x: 2, y: 2, z: 4, core: 2. Of those that a mesh axis runs over, the one named last changes fastest.
Arguments:
- hidden_in: bfloat16 [8, 2048, 1024], P('fsdp', 'ctx'), may hold values from -6 to 6
- cotangent: bfloat16 [8, 2048, 1024], P('fsdp', 'ctx'), may hold values from -6 to 6
- lengths: int32 [8], P('fsdp'), may hold values from 512 to 2048, as said below
- block_of: int32 [4, 2], replicated, may hold values from 0 to 7, as said below
- w_qkv: bfloat16 [1024, 3072], P('fsdp'), may hold values from -0.1875 to 0.1875
- w_attn: bfloat16 [1024, 1024], P('fsdp'), may hold values from -0.1875 to 0.1875
- w_up: bfloat16 [1024, 4096], P('fsdp'), may hold values from -0.1875 to 0.1875
- w_down: bfloat16 [4096, 1024], P('fsdp'), may hold values from -0.09375 to 0.09375
- norm_gains: bfloat16 [1024, 4], P('fsdp'), may hold values from 0.5 to 1.5
Outputs:
- output: bfloat16 [8, 2048, 1024], P('fsdp', 'ctx')
- input_grad: float32 [8, 2048, 1024], P('fsdp', 'ctx')
- qkv_grad: float32 [1024, 3072], P('fsdp')
- attn_out_grad: float32 [1024, 1024], P('fsdp')
- up_grad: float32 [1024, 4096], P('fsdp')
- down_grad: float32 [4096, 1024], P('fsdp')
- gains_grad: float32 [1024, 4], P('fsdp')
Inputs may be any that keep to these rules, and one draw needn't show every extreme that they name: `lengths`: valid positions of each slot, counted from position 0; some slot is full in every draw. `block_of`: row c gives the blocks of 256 positions whose rows ctx index c holds, in that order; the two of a row sum to 7 and every block appears once.
All inputs are finite; a program needn't handle non-finite values.
Results may differ from a plain program's by a relative error of at most 0.014.
Values may be sent and summed in bfloat16 or wider, within the bound.
No kernel may reach another device: no remote copies, remote signals or barrier semaphores. Data moves between devices by JAX's collectives and lax.ppermute only.
A program may use at most 192 MiB of HBM per device.

v0:
```python
from functools import partial
import math

import jax
import jax.numpy as jnp
from jax import lax
from jax.sharding import PartitionSpec as P

D = 1024
HEADS = 16
HEAD_DIM = 64


def layer_norm(values, gain_vec):
    average = jnp.mean(values, axis=-1, keepdims=True)
    centered = values - average
    variance = jnp.mean(centered * centered, axis=-1, keepdims=True)
    return centered * lax.rsqrt(variance + 1e-05) * gain_vec


def angle_tables(positions):
    half_dim = HEAD_DIM // 2
    counter = jnp.arange(half_dim, dtype=jnp.float32)
    inverse = jnp.exp(counter * (-2.0 * math.log(10000.0) / HEAD_DIM))
    angles = positions.astype(jnp.float32)[:, None] * inverse[None, :]
    return (jnp.cos(angles)[:, None, :], jnp.sin(angles)[:, None, :])


def rotate(values, positions):
    cosine, sine_part = angle_tables(positions)
    half_dim = HEAD_DIM // 2
    leading = values[..., :half_dim]
    trailing = values[..., half_dim:]
    return jnp.concatenate(
        [leading * cosine - trailing * sine_part, trailing * cosine + leading * sine_part], axis=-1
    )


def unrotate(values, positions):
    cosine, sine_part = angle_tables(positions)
    half_dim = HEAD_DIM // 2
    leading = values[..., :half_dim]
    trailing = values[..., half_dim:]
    return jnp.concatenate(
        [leading * cosine + trailing * sine_part, trailing * cosine - leading * sine_part], axis=-1
    )


def outer_sum(left, right):
    return lax.dot_general(
        left, right, (((0,), (0,)), ((), ())), preferred_element_type=jnp.float32
    )


def times_transposed(left, right):
    return lax.dot_general(
        left, right, (((1,), (1,)), ((), ())), preferred_element_type=jnp.float32
    )


def gather_weights(w_qkv, w_attn, w_up, w_down, norm_gains):
    return (
        lax.all_gather(w_qkv, "fsdp", axis=0, tiled=True),
        lax.all_gather(w_attn, "fsdp", axis=0, tiled=True),
        lax.all_gather(w_up, "fsdp", axis=0, tiled=True),
        lax.all_gather(w_down, "fsdp", axis=0, tiled=True),
        lax.all_gather(norm_gains, "fsdp", axis=0, tiled=True),
    )


def scan_blocks(step, initial, items):

    def guarded(carry, item):
        return step(carry, item)

    return lax.scan(guarded, initial, items)


def block_scores(queries, key_block, block_pos, query_pos, length):
    scores = (
        jnp.einsum("qhd,khd->hqk", queries, key_block, preferred_element_type=jnp.float32) * 0.125
    )
    allowed = (block_pos[None, :] <= query_pos[:, None]) & (block_pos[None, :] < length)
    return (scores, allowed[None])


def key_items(keys_all, values_all, key_pos, half_rows):
    return (
        keys_all.reshape(-1, half_rows, HEADS, HEAD_DIM),
        values_all.reshape(-1, half_rows, HEADS, HEAD_DIM),
        key_pos.reshape(-1, half_rows),
    )


def forward(gathered, hidden_f, query_pos, key_pos, length):
    w_qkv, w_attn, w_up, w_down, gains_all = gathered
    gains_f = gains_all.astype(jnp.float32)
    tok_rows = hidden_f.shape[0]
    half_rows = tok_rows // 2
    normed = layer_norm(hidden_f, gains_f[:, 0]).astype(jnp.bfloat16)
    mixed = jnp.dot(normed, w_qkv, preferred_element_type=jnp.float32)
    queries = rotate(mixed[:, :D].reshape(tok_rows, HEADS, HEAD_DIM), query_pos).astype(
        jnp.bfloat16
    )
    keys_own = rotate(mixed[:, D : 2 * D].reshape(tok_rows, HEADS, HEAD_DIM), query_pos).astype(
        jnp.bfloat16
    )
    values_own = mixed[:, 2 * D :].reshape(tok_rows, HEADS, HEAD_DIM).astype(jnp.bfloat16)
    keys_all, values_all = (
        lax.all_gather(keys_own, "ctx", axis=0, tiled=True),
        lax.all_gather(values_own, "ctx", axis=0, tiled=True),
    )
    items = key_items(keys_all, values_all, key_pos, half_rows)

    def forward_first_pass(carry, item):
        running_top, running_sum = carry
        key_block, value_block, block_pos = item
        scores, allowed = block_scores(queries, key_block, block_pos, query_pos, length)
        masked = jnp.where(allowed, scores, -1e30)
        new_top = jnp.maximum(running_top, jnp.max(masked, axis=-1))
        rescaled = running_sum * jnp.exp(running_top - new_top)
        added = jnp.sum(jnp.where(allowed, jnp.exp(masked - new_top[..., None]), 0.0), axis=-1)
        return ((new_top, rescaled + added), None)

    start_state = (
        jnp.full((HEADS, tok_rows), -1e30, jnp.float32),
        jnp.zeros((HEADS, tok_rows), jnp.float32),
    )
    (top_all, sum_all), ignored = scan_blocks(forward_first_pass, start_state, items)
    log_total = top_all + jnp.log(sum_all)

    def forward_second_pass(carry, item):
        key_block, value_block, block_pos = item
        scores, allowed = block_scores(queries, key_block, block_pos, query_pos, length)
        probs = jnp.where(allowed, jnp.exp(scores - log_total[..., None]), 0.0).astype(jnp.bfloat16)
        return (
            carry
            + jnp.einsum("hqk,khd->qhd", probs, value_block, preferred_element_type=jnp.float32),
            None,
        )

    attended, ignored = scan_blocks(
        forward_second_pass, jnp.zeros((tok_rows, HEADS, HEAD_DIM), jnp.float32), items
    )
    attended = attended.reshape(tok_rows, D).astype(jnp.bfloat16)
    branch = jnp.dot(attended, w_attn, preferred_element_type=jnp.float32)
    middle = hidden_f + layer_norm(branch, gains_f[:, 1])
    normed_mid = layer_norm(middle, gains_f[:, 2]).astype(jnp.bfloat16)
    lifted = jnp.dot(normed_mid, w_up, preferred_element_type=jnp.float32)
    activated = jax.nn.gelu(lifted, approximate=True).astype(jnp.bfloat16)
    lowered = jnp.dot(activated, w_down, preferred_element_type=jnp.float32)
    result = middle + layer_norm(lowered, gains_f[:, 3])
    return (
        normed,
        queries,
        keys_all,
        values_all,
        log_total,
        attended,
        branch,
        middle,
        normed_mid,
        lifted,
        activated,
        lowered,
        result,
    )


def attention_back(queries, keys_all, values_all, log_total, grad_out, query_pos, key_pos, length):
    tok_rows = queries.shape[0]
    half_rows = tok_rows // 2
    items = key_items(keys_all, values_all, key_pos, half_rows)

    def attention_first_pass(carry, item):
        key_block, value_block, block_pos = item
        scores, allowed = block_scores(queries, key_block, block_pos, query_pos, length)
        probs = jnp.where(allowed, jnp.exp(scores - log_total[..., None]), 0.0)
        grad_probs = jnp.einsum(
            "qhd,khd->hqk", grad_out, value_block, preferred_element_type=jnp.float32
        )
        return (carry + jnp.sum(probs * grad_probs, axis=-1), None)

    inner, ignored = scan_blocks(
        attention_first_pass, jnp.zeros((HEADS, tok_rows), jnp.float32), items
    )

    def attention_second_pass(carry, item):
        key_block, value_block, block_pos = item
        scores, allowed = block_scores(queries, key_block, block_pos, query_pos, length)
        probs = jnp.where(allowed, jnp.exp(scores - log_total[..., None]), 0.0)
        grad_probs = jnp.einsum(
            "qhd,khd->hqk", grad_out, value_block, preferred_element_type=jnp.float32
        )
        grad_scores = (probs * (grad_probs - inner[..., None])).astype(jnp.bfloat16)
        grad_query = (
            jnp.einsum("hqk,khd->qhd", grad_scores, key_block, preferred_element_type=jnp.float32)
            * 0.125
        )
        key_grad = (
            jnp.einsum("hqk,qhd->khd", grad_scores, queries, preferred_element_type=jnp.float32)
            * 0.125
        )
        value_grad = jnp.einsum(
            "hqk,qhd->khd", probs.astype(jnp.bfloat16), grad_out, preferred_element_type=jnp.float32
        )
        return (carry + grad_query, (key_grad, value_grad))

    grad_queries, (key_grads, value_grads) = scan_blocks(
        attention_second_pass, jnp.zeros((tok_rows, HEADS, HEAD_DIM), jnp.float32), items
    )
    return (grad_queries, key_grads.reshape(-1, D), value_grads.reshape(-1, D))


def per_device(hidden_in, cotangent, lengths, block_of, w_qkv, w_attn, w_up, w_down, norm_gains):
    tok_rows = hidden_in.shape[1]
    half_rows = tok_rows // 2
    here = lax.axis_index("ctx")
    block_list = block_of.reshape(-1)
    offsets = jnp.arange(half_rows, dtype=jnp.int32)
    key_pos = (block_list[:, None] * half_rows + offsets[None, :]).reshape(-1)
    own_blocks = lax.dynamic_slice_in_dim(block_list, here * 2, 2, 0)
    query_pos = (own_blocks[:, None] * half_rows + offsets[None, :]).reshape(-1)
    length = lengths[0]
    hidden_f = hidden_in[0].astype(jnp.float32)
    gathered = gather_weights(w_qkv, w_attn, w_up, w_down, norm_gains)
    state = forward(gathered, hidden_f, query_pos, key_pos, length)
    result = state[12]
    (
        normed,
        queries,
        keys_all,
        values_all,
        log_total,
        attended,
        branch,
        middle,
        normed_mid,
        lifted,
        activated,
        lowered,
        ignored,
    ) = state
    w_qkv_all, w_attn_all, w_up_all, w_down_all, gains_all = gathered
    gains_f = gains_all.astype(jnp.float32)
    live_rows = (query_pos < length).astype(jnp.float32)[:, None]
    upstream = cotangent[0].astype(jnp.float32) * live_rows
    ignored, norm_back3 = jax.vjp(layer_norm, lowered, gains_f[:, 3])
    grad_lowered, gain_grad3 = norm_back3(upstream)
    grad_lowered = grad_lowered.astype(jnp.bfloat16)
    grad_down = outer_sum(activated, grad_lowered)
    grad_activated = times_transposed(grad_lowered, w_down_all)
    ignored, gelu_back = jax.vjp(partial(jax.nn.gelu, approximate=True), lifted)
    grad_lifted = gelu_back(grad_activated)[0].astype(jnp.bfloat16)
    grad_up = outer_sum(normed_mid, grad_lifted)
    grad_normed_mid = times_transposed(grad_lifted, w_up_all)
    ignored, norm_back2 = jax.vjp(layer_norm, middle, gains_f[:, 2])
    middle_part, gain_grad2 = norm_back2(grad_normed_mid)
    grad_middle = upstream + middle_part
    ignored, norm_back1 = jax.vjp(layer_norm, branch, gains_f[:, 1])
    grad_branch, gain_grad1 = norm_back1(grad_middle)
    grad_branch = grad_branch.astype(jnp.bfloat16)
    grad_attn = outer_sum(attended, grad_branch)
    grad_attended = times_transposed(grad_branch, w_attn_all).astype(jnp.bfloat16)
    grad_attended = grad_attended.reshape(tok_rows, HEADS, HEAD_DIM)
    grad_queries, key_grads, value_grads = attention_back(
        queries, keys_all, values_all, log_total, grad_attended, query_pos, key_pos, length
    )
    own_key_grads, own_value_grads = (
        lax.psum_scatter(key_grads, "ctx", scatter_dimension=0, tiled=True),
        lax.psum_scatter(value_grads, "ctx", scatter_dimension=0, tiled=True),
    )
    grad_queries = unrotate(grad_queries, query_pos).reshape(tok_rows, D)
    grad_keys = unrotate(own_key_grads.reshape(tok_rows, HEADS, HEAD_DIM), query_pos).reshape(
        tok_rows, D
    )
    grad_mixed = jnp.concatenate([grad_queries, grad_keys, own_value_grads], axis=1).astype(
        jnp.bfloat16
    )
    grad_qkv = outer_sum(normed, grad_mixed)
    grad_normed = times_transposed(grad_mixed, w_qkv_all)
    ignored, norm_back0 = jax.vjp(layer_norm, hidden_f, gains_f[:, 0])
    input_part, gain_grad0 = norm_back0(grad_normed)
    grad_hidden = grad_middle + input_part
    grad_gains = jnp.stack([gain_grad0, gain_grad1, gain_grad2, gain_grad3], axis=1)
    summed = (
        lax.psum_scatter(grad_qkv, "fsdp", scatter_dimension=0, tiled=True),
        lax.psum_scatter(grad_attn, "fsdp", scatter_dimension=0, tiled=True),
        lax.psum_scatter(grad_up, "fsdp", scatter_dimension=0, tiled=True),
        lax.psum_scatter(grad_down, "fsdp", scatter_dimension=0, tiled=True),
        lax.psum_scatter(grad_gains, "fsdp", scatter_dimension=0, tiled=True),
    )
    totals = lax.psum((summed[0], summed[1], summed[2], summed[3], summed[4]), "ctx")
    return (
        result.astype(jnp.bfloat16)[None],
        grad_hidden[None],
        totals[0],
        totals[1],
        totals[2],
        totals[3],
        totals[4],
    )


def solution(mesh):
    in_specs = (
        P("fsdp", "ctx", None),
        P("fsdp", "ctx", None),
        P("fsdp"),
        P(),
        P("fsdp", None),
        P("fsdp", None),
        P("fsdp", None),
        P("fsdp", None),
        P("fsdp", None),
    )
    out_specs = (
        P("fsdp", "ctx", None),
        P("fsdp", "ctx", None),
        P("fsdp", None),
        P("fsdp", None),
        P("fsdp", None),
        P("fsdp", None),
        P("fsdp", None),
    )
    return jax.shard_map(
        per_device, mesh=mesh, in_specs=in_specs, out_specs=out_specs, check_vma=False
    )
```

profile of v0, /device:TPU:0, one launch (start us, length us, event | category | flops | bytes accessed | tf_op | source)
XLA Modules:
  0.0 2369.0 jit_solution(6167322480907268838)
XLA Ops:
  34.5 77.4 %all-gather.7.cloned.1.call-done = bf16[1024,3072]{1,0:T(8,128)(2,1)} async-done(((bf16[128,3072]{1,0:T(8,128)(2,1)}), bf16[1024,3072]{1,0:T(8,128)(2,1)}) %all-gather.7.cloned.1.call-update) | async-done | bytes 6291472 | tf_op jit(solution)/shard_map/all_gather | solution.py:63
  137.9 25.6 %all-gather.11.cloned.1.call-done = bf16[2048,16,64]{0,2,1:T(8,128)(2,1)} async-done(((bf16[512,16,64]{0,2,1:T(8,128)(2,1)}), bf16[2048,16,64]{0,2,1:T(8,128)(2,1)}) %all-gather.11.cloned.1.call-update) | async-done | bytes 4194320 | tf_op jit(solution)/shard_map/all_gather | solution.py:110
  168.2 44.4 %while.50 = (s32[]{:T(128)}, f32[16,512]{1,0:T(8,128)S(1)}, f32[16,512]{1,0:T(8,128)S(1)}, s32[8,256]{1,0:T(8,128)S(1)}, s32[]{:T(128)}, /*index=5*/bf16[8,256,1...) while((s32[]{:T(128)}, f32[16,512]{1,0:T(8,128)S(1)}, ...), condition=%wide.region_5.6_spmd.clone, body=%wide.region_2.5_spmd.clone.sunk | while | flops 285516544 | bytes 19181196 | solution.py:76
  217.4 39.4 %while.51 = (s32[]{:T(128)}, f32[512,16,64]{0,2,1:T(8,128)S(1)}, bf16[8,256,16,64]{1,3,2,0:T(8,128)(2,1)}, s32[8,256]{1,0:T(8,128)S(1)}, s32[]{:T(128)}, /*index...) while((s32[]{:T(128)}, f32[512,16,64]{0,2,1:T(8,128)S(1)}, ...), condition=%wide.region_7.8_spmd.clone, body=%wide.region_6.7_spmd.clone.sunk | while | flops 546571008 | bytes 6599822 | solution.py:76
  265.2 111.9 %all-gather.15.cloned.1.call-done = bf16[1024,4096]{1,0:T(8,128)(2,1)} async-done(((bf16[128,4096]{1,0:T(8,128)(2,1)}), bf16[1024,4096]{1,0:T(8,128)(2,1)}) %all-gather.15.cloned.1.call-update) | async-done | bytes 8388624 | tf_op jit(solution)/shard_map/all_gather | solution.py:65
  388.9 113.3 %all-gather.17.cloned.1.call-done = bf16[4096,1024]{1,0:T(8,128)(2,1)} async-done(((bf16[512,1024]{1,0:T(8,128)(2,1)}), bf16[4096,1024]{1,0:T(8,128)(2,1)}) %all-gather.17.cloned.1.call-update) | async-done | bytes 8388624 | tf_op jit(solution)/shard_map/all_gather | solution.py:66
  548.6 60.9 %while.52 = (s32[]{:T(128)}, f32[16,512]{1,0:T(8,128)S(1)}, s32[8,256]{1,0:T(8,128)S(1)}, s32[]{:T(128)}, bf16[8,256,16,64]{1,3,2,0:T(8,128)(2,1)}, /*index=5*/b...) while((s32[]{:T(128)}, f32[16,512]{1,0:T(8,128)S(1)}, ...), condition=%wide.region_22.23_spmd.clone, body=%wide.region_20.22_spmd.clone.sunk | while | flops 547627776 | bytes 20360860 | solution.py:76
  609.5 529.2 %while.53 = (s32[]{:T(128)}, f32[512,16,64]{0,2,1:T(8,128)}, f32[8,256,16,64]{1,0,3,2:T(8,128)}, f32[8,256,16,64]{1,0,3,2:T(8,128)}, bf16[8,256,16,64]{1,3,2,0:T...) while((s32[]{:T(128)}, f32[512,16,64]{0,2,1:T(8,128)}, ...), condition=%wide.region_24.25_spmd.clone, body=%wide.region_23.24_spmd.clone.sunk | while | flops 1365246720 | bytes 75476720 | solution.py:76
  627.2 24.3 %dynamic_update_slice.11 = f32[8,256,16,64]{1,0,3,2:T(8,128)} dynamic-update-slice(f32[8,256,16,64]{1,0,3,2:T(8,128)} %get-tuple-element.1009, f32[1,256,16,64]{1,0,3,2:T(1,128)S(1)} %copy.121, s32[]{:T(128)S(6)} %copy.150, s32[]{:T(128)} %constant.98.clone.1..sunk.3, s32[]{:T(128)} %constant.98.clone.1..sunk.3, s32[]{:T(128)} %constant.98.clone.1..sunk.3) | dynamic-update-slice | bytes 2097156 | tf_op jit(solution)/shard_map/while/body/jit(dynamic_update_index_in_dim)/dynamic_update_slice | solution.py:76
  651.5 24.2 %dynamic_update_slice.12 = f32[8,256,16,64]{1,0,3,2:T(8,128)} dynamic-update-slice(f32[8,256,16,64]{1,0,3,2:T(8,128)} %get-tuple-element.1010, f32[1,256,16,64]{1,0,3,2:T(1,128)S(1)} %copy.122, s32[]{:T(128)S(6)} %copy.150, s32[]{:T(128)} %constant.98.clone.1..sunk.3, s32[]{:T(128)} %constant.98.clone.1..sunk.3, s32[]{:T(128)} %constant.98.clone.1..sunk.3) | dynamic-update-slice | bytes 2097156 | tf_op jit(solution)/shard_map/while/body/jit(dynamic_update_index_in_dim)/dynamic_update_slice | solution.py:76
  693.3 24.3 %dynamic_update_slice.11 = f32[8,256,16,64]{1,0,3,2:T(8,128)} dynamic-update-slice(f32[8,256,16,64]{1,0,3,2:T(8,128)} %get-tuple-element.1009, f32[1,256,16,64]{1,0,3,2:T(1,128)S(1)} %copy.121, s32[]{:T(128)S(6)} %copy.150, s32[]{:T(128)} %constant.98.clone.1..sunk.3, s32[]{:T(128)} %constant.98.clone.1..sunk.3, s32[]{:T(128)} %constant.98.clone.1..sunk.3) | dynamic-update-slice | bytes 2097156 | tf_op jit(solution)/shard_map/while/body/jit(dynamic_update_index_in_dim)/dynamic_update_slice | solution.py:76
  759.4 24.3 %dynamic_update_slice.11 = f32[8,256,16,64]{1,0,3,2:T(8,128)} dynamic-update-slice(f32[8,256,16,64]{1,0,3,2:T(8,128)} %get-tuple-element.1009, f32[1,256,16,64]{1,0,3,2:T(1,128)S(1)} %copy.121, s32[]{:T(128)S(6)} %copy.150, s32[]{:T(128)} %constant.98.clone.1..sunk.3, s32[]{:T(128)} %constant.98.clone.1..sunk.3, s32[]{:T(128)} %constant.98.clone.1..sunk.3) | dynamic-update-slice | bytes 2097156 | tf_op jit(solution)/shard_map/while/body/jit(dynamic_update_index_in_dim)/dynamic_update_slice | solution.py:76
  825.5 24.3 %dynamic_update_slice.11 = f32[8,256,16,64]{1,0,3,2:T(8,128)} dynamic-update-slice(f32[8,256,16,64]{1,0,3,2:T(8,128)} %get-tuple-element.1009, f32[1,256,16,64]{1,0,3,2:T(1,128)S(1)} %copy.121, s32[]{:T(128)S(6)} %copy.150, s32[]{:T(128)} %constant.98.clone.1..sunk.3, s32[]{:T(128)} %constant.98.clone.1..sunk.3, s32[]{:T(128)} %constant.98.clone.1..sunk.3) | dynamic-update-slice | bytes 2097156 | tf_op jit(solution)/shard_map/while/body/jit(dynamic_update_index_in_dim)/dynamic_update_slice | solution.py:76
  891.6 24.3 %dynamic_update_slice.11 = f32[8,256,16,64]{1,0,3,2:T(8,128)} dynamic-update-slice(f32[8,256,16,64]{1,0,3,2:T(8,128)} %get-tuple-element.1009, f32[1,256,16,64]{1,0,3,2:T(1,128)S(1)} %copy.121, s32[]{:T(128)S(6)} %copy.150, s32[]{:T(128)} %constant.98.clone.1..sunk.3, s32[]{:T(128)} %constant.98.clone.1..sunk.3, s32[]{:T(128)} %constant.98.clone.1..sunk.3) | dynamic-update-slice | bytes 2097156 | tf_op jit(solution)/shard_map/while/body/jit(dynamic_update_index_in_dim)/dynamic_update_slice | solution.py:76
  957.7 24.3 %dynamic_update_slice.11 = f32[8,256,16,64]{1,0,3,2:T(8,128)} dynamic-update-slice(f32[8,256,16,64]{1,0,3,2:T(8,128)} %get-tuple-element.1009, f32[1,256,16,64]{1,0,3,2:T(1,128)S(1)} %copy.121, s32[]{:T(128)S(6)} %copy.150, s32[]{:T(128)} %constant.98.clone.1..sunk.3, s32[]{:T(128)} %constant.98.clone.1..sunk.3, s32[]{:T(128)} %constant.98.clone.1..sunk.3) | dynamic-update-slice | bytes 2097156 | tf_op jit(solution)/shard_map/while/body/jit(dynamic_update_index_in_dim)/dynamic_update_slice | solution.py:76
  1023.8 24.3 %dynamic_update_slice.11 = f32[8,256,16,64]{1,0,3,2:T(8,128)} dynamic-update-slice(f32[8,256,16,64]{1,0,3,2:T(8,128)} %get-tuple-element.1009, f32[1,256,16,64]{1,0,3,2:T(1,128)S(1)} %copy.121, s32[]{:T(128)S(6)} %copy.150, s32[]{:T(128)} %constant.98.clone.1..sunk.3, s32[]{:T(128)} %constant.98.clone.1..sunk.3, s32[]{:T(128)} %constant.98.clone.1..sunk.3) | dynamic-update-slice | bytes 2097156 | tf_op jit(solution)/shard_map/while/body/jit(dynamic_update_index_in_dim)/dynamic_update_slice | solution.py:76
  1089.9 24.3 %dynamic_update_slice.11 = f32[8,256,16,64]{1,0,3,2:T(8,128)} dynamic-update-slice(f32[8,256,16,64]{1,0,3,2:T(8,128)} %get-tuple-element.1009, f32[1,256,16,64]{1,0,3,2:T(1,128)S(1)} %copy.121, s32[]{:T(128)S(6)} %copy.150, s32[]{:T(128)} %constant.98.clone.1..sunk.3, s32[]{:T(128)} %constant.98.clone.1..sunk.3, s32[]{:T(128)} %constant.98.clone.1..sunk.3) | dynamic-update-slice | bytes 2097156 | tf_op jit(solution)/shard_map/while/body/jit(dynamic_update_index_in_dim)/dynamic_update_slice | solution.py:76
  1221.1 72.8 %reduce-scatter.10.cloned.1.call-done = f32[512,1024]{0,1:T(8,128)} async-done(((f32[2048,1024]{0,1:T(8,128)}), f32[512,1024]{0,1:T(8,128)}) %reduce-scatter.10.cloned.1.call-update) | async-done | bytes 2097168 | tf_op jit(solution)/shard_map/reduce_scatter | solution.py:270
  1316.7 68.9 %reduce-scatter.16.cloned.1.call-done = f32[128,1024]{1,0:T(8,128)} async-done(((f32[1024,1024]{1,0:T(8,128)}), f32[128,1024]{1,0:T(8,128)}) %reduce-scatter.16.cloned.1.call-update) | async-done | bytes 524304 | tf_op jit(solution)/shard_map/reduce_scatter | solution.py:288
  1385.5 286.6 %reduce-scatter.20.cloned.1.call-done = f32[512,1024]{1,0:T(8,128)} async-done(((f32[4096,1024]{1,0:T(8,128)}), f32[512,1024]{1,0:T(8,128)}) %reduce-scatter.20.cloned.1.call-update) | async-done | bytes 2097168 | tf_op jit(solution)/shard_map/reduce_scatter | solution.py:290
  1672.2 285.6 %reduce-scatter.18.cloned.1.call-done = f32[128,4096]{1,0:T(8,128)} async-done(((f32[1024,4096]{1,0:T(8,128)}), f32[128,4096]{1,0:T(8,128)}) %reduce-scatter.18.cloned.1.call-update) | async-done | bytes 2097168 | tf_op jit(solution)/shard_map/reduce_scatter | solution.py:289
  1957.7 210.3 %reduce-scatter.14.cloned.1.call-done = f32[128,3072]{1,0:T(8,128)} async-done(((f32[1024,3072]{1,0:T(8,128)}), f32[128,3072]{1,0:T(8,128)}) %reduce-scatter.14.cloned.1.call-update) | async-done | bytes 1572880 | tf_op jit(solution)/shard_map/reduce_scatter | solution.py:287
  2173.4 59.9 %reduce-scatter.22.cloned.1.call-done = f32[128,4]{1,0:T(8,128)} async-done(((f32[1024,4]{1,0:T(8,128)}), f32[128,4]{1,0:T(8,128)}) %reduce-scatter.22.cloned.1.call-update) | async-done | bytes 2064
  2240.4 114.5 %all-reduce.3.cloned.1.call-done = (f32[128,3072]{1,0:T(8,128)}, f32[128,1024]{1,0:T(8,128)}, f32[128,4096]{1,0:T(8,128)}, f32[512,1024]{1,0:T(8,128)}) async-done(((f32[128,3072]{1,0:T(8,128)}, f32[128,1024]{1,0:T(8,128)}, f32[128,4096]{1,0:T(8,128)}, f32[512,1024]{1,0:T(8,128)}), (f32[128,3072]{1,0:T(8,128)}, f32[128,1024]{1,0:T(8,128)}, f32[128,4096]{1,0:T(8,128)}, ...) | async-done | bytes 6291472 | tf_op jit(solution)/shard_map/psum | solution.py:293
  (518 shorter events, 706.1 us)
Async XLA Ops:
  7.2 104.8 %all-gather.7.cloned.1.call-start = ((), (), s32[]{:S(2)}) async-start(), calls=%async_computation.7 | async-start | bytes 7077888 | tf_op jit(solution)/shard_map/all_gather | solution.py:63
  7.9 155.6 %all-gather.11.cloned.1.call-start = ((), (), s32[]{:S(2)}) async-start(), calls=%async_computation.9 | async-start | bytes 5242880 | tf_op jit(solution)/shard_map/all_gather | solution.py:110
  33.1 84.6 %copy-start.33 = (f32[512]{0:T(512)}, f32[512]{0:T(512)S(1)}, u32[]{:S(2)}) copy-start(f32[512]{0:T(512)S(1)} %broadcast_multiply_fusion.3) | copy-start | bytes 6148
  34.2 507.1 %copy-start.45 = (f32[1024,1]{0,1:T(1,128)}, f32[1024,1]{0,1:T(1,128)S(1)}, u32[]{:S(2)}) copy-start(f32[1024,1]{0,1:T(1,128)S(1)} %get-tuple-element.615) | copy-start | bytes 12292
  34.5 92.0 %copy-start.24 = (f32[512,32]{0,1:T(8,128)}, f32[512,32]{0,1:T(8,128)S(1)}, u32[]{:S(2)}) copy-start(f32[512,32]{0,1:T(8,128)S(1)} %get-tuple-element.618) | copy-start | bytes 196612
  34.5 92.0 %copy-start.26 = (f32[512,32]{0,1:T(8,128)}, f32[512,32]{0,1:T(8,128)S(1)}, u32[]{:S(2)}) copy-start(f32[512,32]{0,1:T(8,128)S(1)} %get-tuple-element.619) | copy-start | bytes 196612
  130.7 82.0 %all-gather.9.cloned.1.call-start = ((), (), s32[]{:S(2)}) async-start(), calls=%async_computation.8 | async-start | bytes 5242880 | tf_op jit(solution)/shard_map/all_gather | solution.py:111
  133.9 124.0 %all-gather.13.cloned.1.call-start = ((), (), s32[]{:S(2)}) async-start(), calls=%async_computation.10 | async-start | bytes 2359296 | tf_op jit(solution)/shard_map/all_gather | solution.py:64
  134.4 242.6 %all-gather.15.cloned.1.call-start = ((), (), s32[]{:S(2)}) async-start(), calls=%async_computation.11 | async-start | bytes 9437184 | tf_op jit(solution)/shard_map/all_gather | solution.py:65
  135.0 367.2 %all-gather.17.cloned.1.call-start = ((), (), s32[]{:S(2)}) async-start(), calls=%async_computation.12 | async-start | bytes 9437184 | tf_op jit(solution)/shard_map/all_gather | solution.py:66
  135.6 1083.8 %reduce-scatter.12.cloned.1.call-start = ((), (), s32[]{:S(2)}) async-start(), calls=%async_computation.14 | async-start | bytes 10485760 | tf_op jit(solution)/shard_map/reduce_scatter | solution.py:271
  136.5 407.1 %copy-start.29 = (f32[1,2,2,128]{3,1,2,0:T(2,128)}, f32[1,2,2,128]{3,1,2,0:T(2,128)S(1)}, u32[]{:S(2)}) copy-start(f32[1,2,2,128]{3,1,2,0:T(2,128)S(1)} %copy.104) | copy-start | bytes 6148
  263.5 277.7 %copy-start.39 = (f32[512]{0:T(512)}, f32[512]{0:T(512)S(1)}, u32[]{:S(2)}) copy-start(f32[512]{0:T(512)S(1)} %broadcast_multiply_fusion.1) | copy-start | bytes 6148
  265.2 276.1 %copy-start.47 = (f32[512]{0:T(512)}, f32[512]{0:T(512)S(1)}, u32[]{:S(2)}) copy-start(f32[512]{0:T(512)S(1)} %fusion.96) | copy-start | bytes 6148
  1149.4 144.6 %reduce-scatter.10.cloned.1.call-start = ((), (), s32[]{:S(2)}) async-start(), calls=%async_computation.13 | async-start | bytes 10485760 | tf_op jit(solution)/shard_map/reduce_scatter | solution.py:270
  1161.8 223.7 %reduce-scatter.16.cloned.1.call-start = ((), (), s32[]{:S(2)}) async-start(), calls=%async_computation.16 | async-start | bytes 4718592 | tf_op jit(solution)/shard_map/reduce_scatter | solution.py:288
  1167.3 504.8 %reduce-scatter.20.cloned.1.call-start = ((), (), s32[]{:S(2)}) async-start(), calls=%async_computation.18 | async-start | bytes 18874368 | tf_op jit(solution)/shard_map/reduce_scatter | solution.py:290
  1184.8 773.0 %reduce-scatter.18.cloned.1.call-start = ((), (), s32[]{:S(2)}) async-start(), calls=%async_computation.17 | async-start | bytes 18874368 | tf_op jit(solution)/shard_map/reduce_scatter | solution.py:289
  1197.0 96.9 %copy-start.2 = (f32[512,16,64]{0,2,1:T(8,128)S(1)}, f32[512,16,64]{0,2,1:T(8,128)}, u32[]{:S(2)}) copy-start(f32[512,16,64]{0,2,1:T(8,128)} %get-tuple-element.222) | copy-start | bytes 6291460
  1197.0 96.9 %copy-start.25 = (f32[512,32]{0,1:T(8,128)S(1)}, f32[512,32]{0,1:T(8,128)}, u32[]{:S(2)}) copy-start(f32[512,32]{0,1:T(8,128)} %copy-done.24) | copy-start | bytes 196612
  1197.0 96.9 %copy-start.27 = (f32[512,32]{0,1:T(8,128)S(1)}, f32[512,32]{0,1:T(8,128)}, u32[]{:S(2)}) copy-start(f32[512,32]{0,1:T(8,128)} %copy-done.26) | copy-start | bytes 196612
  1197.0 970.9 %reduce-scatter.14.cloned.1.call-start = ((), (), s32[]{:S(2)}) async-start(), calls=%async_computation.15 | async-start | bytes 14155776 | tf_op jit(solution)/shard_map/reduce_scatter | solution.py:287
  1307.2 926.1 %reduce-scatter.22.cloned.1.call-start = ((), (), s32[]{:S(2)}) async-start(), calls=%async_computation.19 | async-start | bytes 589824
  1316.6 1038.3 %all-reduce.3.cloned.1.call-start = ((), (), s32[]{:S(2)}) async-start(), calls=%async_computation.20 | async-start | bytes 12582912 | tf_op jit(solution)/shard_map/psum | solution.py:293
  (58 other events, 347.6 us)
Sparse Core Ops, SparseCore 0:
  10.2 101.7 all-gather.6
  130.8 32.6 all-gather.10
  165.7 34.4 all-gather.8
  202.2 49.4 all-gather.12
  253.6 123.4 all-gather.14
  379.0 123.1 all-gather.16
  1149.5 69.8 reduce-scatter.11
  1222.2 71.7 reduce-scatter.9
  1297.6 87.8 reduce-scatter.15
  1389.6 282.4 reduce-scatter.19
  1675.9 281.7 reduce-scatter.17
  1961.6 206.3 reduce-scatter.13
  2172.3 60.9 reduce-scatter.21
  2235.7 119.1 all-reduce.2
where the time goes:
time: 2390 us; the launch traced here: 2370 us
  waiting for transfers between devices  1450 us (61%)
  local copies, waits for them, and re-layouts  487 us (20%)
  matrix products  312 us (13%)
  other arithmetic  71.7 us (3%)
  blocking collectives  28.9 us (1%)
    dynamic_update_slice x32, local copies, waits for them, and re-layouts, scan_blocks(): return lax.scan(guarded, initial, items)  405 us
    reduce_scatter x1, waiting for transfers between devices, per_device(): lax.psum_scatter(grad_down, 'fsdp', scatter_dimension=0, tiled=True)  287 us
    reduce_scatter x1, waiting for transfers between devices, per_device(): lax.psum_scatter(grad_up, 'fsdp', scatter_dimension=0, tiled=True)  286 us
    reduce_scatter x1, waiting for transfers between devices, per_device(): lax.psum_scatter(grad_qkv, 'fsdp', scatter_dimension=0, tiled=True)  210 us
    psum x1, waiting for transfers between devices, per_device(): lax.psum((summed[0], summed[1], summed[2], summed[3], summed[4]), 'ctx')  115 us
    all_gather x1, waiting for transfers between devices, gather_weights(): lax.all_gather(w_down, 'fsdp', axis=0, tiled=True)  113 us
    all_gather x1, waiting for transfers between devices, gather_weights(): lax.all_gather(w_up, 'fsdp', axis=0, tiled=True)  112 us
    all_gather x1, waiting for transfers between devices, gather_weights(): lax.all_gather(w_qkv, 'fsdp', axis=0, tiled=True)  77.4 us
  transfers between devices with their start and end apart: 14, of which 12 were waited for; matrix products, arithmetic and copies ran while one was open for 8% of the time, Pallas kernels for 0%

commit v1 on v0

v1 whole, which is shorter than its diff:
```python
import math

import jax
import jax.numpy as jnp
from jax import lax
from jax.experimental import pallas as pl
from jax.experimental.pallas import tpu as pltpu
from jax.sharding import PartitionSpec as P

HEAD_DIM = 64
BF = jnp.bfloat16
F32 = jnp.float32
NEG = -1e30
EPS = 1e-05


def mm(left, right):
    return jnp.dot(left, right, preferred_element_type=F32)


def mm_tn(left, right):
    return lax.dot_general(left, right, (((0,), (0,)), ((), ())), preferred_element_type=F32)


def mm_nt(left, right):
    return lax.dot_general(left, right, (((1,), (1,)), ((), ())), preferred_element_type=F32)


def swap(value, bit):
    return lax.ppermute(value, "ctx", [(i, i ^ bit) for i in range(4)])


def ring_pairs(n):
    order = list(range(0, n, 2)) + list(range(n - 1, 0, -2))
    ahead = [(order[i], order[(i + 1) % n]) for i in range(n)]
    return ahead, [(b, a) for a, b in ahead]


def ring_owner(place, n):
    place = lax.rem(place + 2 * n, n)
    return jnp.where(place < n // 2, 2 * place, 2 * (n - place) - 1)


def ring_place(me, n):
    return jnp.where(lax.rem(me, 2) == 0, lax.div(me, 2), n - 1 - lax.div(me, 2))


def ring_gather(block, n, flip, store, target):
    ahead, back = ring_pairs(n)
    sign = -1
    if flip:
        ahead, back, sign = back, ahead, 1
    me = lax.axis_index("fsdp")
    place = ring_place(me, n)
    target = store(target, me, block)
    one = two = block
    for step in range(1, n // 2 + 1):
        one = lax.ppermute(one, "fsdp", ahead)
        if step <= (n - 1) // 2:
            two = lax.ppermute(two, "fsdp", back)
        target = store(target, ring_owner(place + sign * step, n), one)
        if step <= (n - 1) // 2:
            target = store(target, ring_owner(place - sign * step, n), two)
    return target


def ring_scatter(pick, n, flip):
    ahead, back = ring_pairs(n)
    sign = 1
    if flip:
        ahead, back, sign = back, ahead, -1
    place = ring_place(lax.axis_index("fsdp"), n)

    def at(offset):
        return pick(ring_owner(place + offset, n))

    far, near = n // 2, (n - 1) // 2
    one, two = at(sign * far), at(-sign * near)
    for step in range(far):
        one = lax.ppermute(one, "fsdp", ahead)
        if step < near:
            two = lax.ppermute(two, "fsdp", back)
        left = far - 1 - step
        if left > 0:
            one = (one.astype(F32) + at(sign * left).astype(F32)).astype(BF)
        left = near - 1 - step
        if left > 0:
            two = (two.astype(F32) + at(-sign * left).astype(F32)).astype(BF)
    return one.astype(F32) + two.astype(F32) + at(0).astype(F32)


def normalize(values):
    average = jnp.mean(values, axis=-1, keepdims=True)
    centered = values - average
    variance = jnp.mean(centered * centered, axis=-1, keepdims=True)
    scale = lax.rsqrt(variance + EPS)
    return centered * scale, scale


def norm_back(unit, scale, gain, incoming):
    weighted = incoming * gain
    return (
        weighted
        - jnp.mean(weighted, axis=-1, keepdims=True)
        - unit * jnp.mean(weighted * unit, axis=-1, keepdims=True)
    ) * scale


def turned(value, cosine, sine_signed, inverse):
    width = value.shape[1]
    lane = lax.broadcasted_iota(jnp.int32, value.shape, 1)
    half = HEAD_DIM // 2
    other = jnp.where(
        lax.rem(lane, HEAD_DIM) < half,
        pltpu.roll(value, width - half, 1),
        pltpu.roll(value, half, 1),
    )
    repeat = width // cosine.shape[1]
    cosine = jnp.concatenate([cosine] * repeat, axis=1)
    sine_signed = jnp.concatenate([sine_signed] * repeat, axis=1)
    if inverse:
        return value * cosine - other * sine_signed
    return value * cosine + other * sine_signed


def project(hidden, weight, gain, cosine, sine_signed):
    rows, dim = hidden.shape
    width = weight.shape[1]
    part = width // 3
    step = 512

    def body(hidden_ref, weight_ref, gain_ref, cos_ref, sin_ref, normed_ref, out_ref):
        unit, _ = normalize(hidden_ref[...].astype(F32))
        normed = (unit * gain_ref[...]).astype(BF)
        normed_ref[...] = normed
        mixed = mm(normed, weight_ref[...])
        cos_part, sin_part = cos_ref[...], sin_ref[...]
        queries = turned(mixed[:, :part], cos_part, sin_part, False).astype(BF)
        out_ref[:, :part] = (queries.astype(F32) * 0.125).astype(BF)
        out_ref[:, part : 2 * part] = turned(
            mixed[:, part : 2 * part], cos_part, sin_part, False
        ).astype(BF)
        out_ref[:, 2 * part :] = mixed[:, 2 * part :].astype(BF)

    return pl.pallas_call(
        body,
        grid=(rows // step,),
        in_specs=[
            pl.BlockSpec((step, dim), lambda i: (i, 0)),
            pl.BlockSpec((dim, width), lambda i: (0, 0)),
            pl.BlockSpec((1, dim), lambda i: (0, 0)),
            pl.BlockSpec((step, 128), lambda i: (i, 0)),
            pl.BlockSpec((step, 128), lambda i: (i, 0)),
        ],
        out_specs=[
            pl.BlockSpec((step, dim), lambda i: (i, 0)),
            pl.BlockSpec((step, width), lambda i: (i, 0)),
        ],
        out_shape=[
            jax.ShapeDtypeStruct((rows, dim), BF),
            jax.ShapeDtypeStruct((rows, width), BF),
        ],
        compiler_params=pltpu.CompilerParams(vmem_limit_bytes=32 << 20),
        cost_estimate=pl.CostEstimate(
            flops=2 * rows * dim * width, bytes_accessed=12 << 20, transcendentals=rows
        ),
        name="project",
    )(hidden, weight, gain, cosine, sine_signed)


def head_masked(value, heads):
    row = lax.broadcasted_iota(jnp.int32, value.shape, 0)
    return [
        jnp.where(lax.div(row, HEAD_DIM) == h, value, 0.0).astype(BF) for h in range(heads)
    ]


def folded(value, op):
    rows, cols = value.shape
    return op(value.reshape(rows // 8, 8, cols), axis=0)


def attention(order, length, qkv, blk):
    rows = qkv.shape[0]
    width = qkv.shape[1] // 3
    heads = width // HEAD_DIM
    nb = rows // blk

    def body(order_ref, length_ref, qkv_ref, out_ref, lse_ref, keys, values_t, q_masked, scores, total):
        live = length_ref[0]

        def fill(p, carry):
            rows_at = pl.ds(pl.multiple_of(order_ref[p] * blk, blk), blk)
            keys[p] = qkv_ref[rows_at, width : 2 * width]
            values_t[p] = jnp.transpose(qkv_ref[rows_at, 2 * width :].astype(F32)).astype(BF)
            return carry

        lax.fori_loop(0, nb, fill, 0)

        def per_block(i, carry):
            rows_at = pl.ds(pl.multiple_of(order_ref[i] * blk, blk), blk)
            query_t = jnp.transpose(qkv_ref[rows_at, :width].astype(F32))
            for h, masked in enumerate(head_masked(query_t, heads)):
                q_masked[h] = masked

            def first(j, tops, masks):
                key_block = keys[j]
                if masks:
                    key_pos = j * blk + lax.broadcasted_iota(jnp.int32, (blk, blk), 0)
                    query_pos = i * blk + lax.broadcasted_iota(jnp.int32, (blk, blk), 1)
                    allowed = (key_pos <= query_pos) & (key_pos < live)
                new = []
                for h in range(heads):
                    s = mm(key_block, q_masked[h])
                    if masks:
                        s = jnp.where(allowed, s, NEG)
                    scores[h, j] = s
                    new.append(jnp.maximum(tops[h], folded(s, jnp.max)))
                return tuple(new)

            whole = jnp.minimum(i, lax.div(live, blk))
            tops = tuple(jnp.full((8, blk), NEG, F32) for _ in range(heads))
            tops = lax.fori_loop(0, whole, lambda j, c: first(j, c, False), tops)
            tops = lax.fori_loop(whole, i + 1, lambda j, c: first(j, c, True), tops)
            tops = [jnp.max(t, axis=0, keepdims=True) for t in tops]
            total[...] = jnp.zeros_like(total)

            def second(j, sums):
                new = []
                for h in range(heads):
                    p = jnp.exp(scores[h, j] - tops[h])
                    new.append(sums[h] + folded(p, jnp.sum))
                    at = slice(h * HEAD_DIM, (h + 1) * HEAD_DIM)
                    total[at, :] += mm(values_t[j, at, :], p.astype(BF))
                return tuple(new)

            sums = tuple(jnp.zeros((8, blk), F32) for _ in range(heads))
            sums = lax.fori_loop(0, i + 1, second, sums)
            scaled = []
            for h in range(heads):
                sum_h = jnp.sum(sums[h], axis=0, keepdims=True)
                lse_ref[i, h : h + 1, :] = tops[h] + jnp.log(sum_h)
                scaled.append(total[h * HEAD_DIM : (h + 1) * HEAD_DIM, :] * (1.0 / sum_h))
            out_ref[rows_at, :] = jnp.transpose(jnp.concatenate(scaled, axis=0)).astype(BF)
            return carry

        lax.fori_loop(0, nb, per_block, 0)

    tiles = nb * (nb + 1) // 2 * heads
    vm = pl.BlockSpec(memory_space=pltpu.VMEM)
    sm = pl.BlockSpec(memory_space=pltpu.SMEM)
    return pl.pallas_call(
        body,
        in_specs=[sm, sm, vm],
        out_specs=[vm, vm],
        out_shape=[
            jax.ShapeDtypeStruct((rows, width), BF),
            jax.ShapeDtypeStruct((nb, 8, blk), F32),
        ],
        scratch_shapes=[
            pltpu.VMEM((nb, blk, width), BF),
            pltpu.VMEM((nb, width, blk), BF),
            pltpu.VMEM((heads, width, blk), BF),
            pltpu.VMEM((heads, nb, blk, blk), F32),
            pltpu.VMEM((width, blk), F32),
        ],
        compiler_params=pltpu.CompilerParams(vmem_limit_bytes=32 << 20),
        cost_estimate=pl.CostEstimate(
            flops=tiles * 8 * blk * blk * width // 4,
            bytes_accessed=5 << 20,
            transcendentals=tiles * blk * blk,
        ),
        name="attention",
    )(order, length, qkv)


def attention_back(order, length, qkv, grad_out, out, lse, cosine, sine_signed, blk):
    rows = qkv.shape[0]
    width = qkv.shape[1] // 3
    heads = width // HEAD_DIM
    nb = rows // blk

    def body(
        order_ref, length_ref, qkv_ref, gout_ref, att_ref, lse_ref, cos_ref, sin_ref, result_ref,
        keys, keys_t, values, q_cols, q_rows, g_cols, g_rows, grad_q, grad_k, grad_v, inner,
    ):
        live = length_ref[0]

        def fill(p, carry):
            rows_at = pl.ds(pl.multiple_of(order_ref[p] * blk, blk), blk)
            key_block = qkv_ref[rows_at, width : 2 * width]
            keys[p] = key_block
            keys_t[p] = jnp.transpose(key_block.astype(F32)).astype(BF)
            values[p] = qkv_ref[rows_at, 2 * width :]
            grad_k[p] = jnp.zeros((blk, width), F32)
            grad_v[p] = jnp.zeros((blk, width), F32)
            return carry

        lax.fori_loop(0, nb, fill, 0)
        lane_head = lax.div(lax.broadcasted_iota(jnp.int32, (blk, width), 1), HEAD_DIM)

        def per_block(i, carry):
            rows_at = pl.ds(pl.multiple_of(order_ref[i] * blk, blk), blk)
            query = qkv_ref[rows_at, :width].astype(F32)
            gout = gout_ref[rows_at, :].astype(F32)
            inner_t = jnp.transpose(gout * att_ref[rows_at, :].astype(F32))
            for h, masked in enumerate(head_masked(jnp.transpose(query), heads)):
                q_cols[h] = masked
            for h, masked in enumerate(head_masked(jnp.transpose(gout), heads)):
                g_cols[h] = masked
            for h in range(heads):
                at = slice(h * blk, (h + 1) * blk)
                q_rows[at, :] = jnp.where(lane_head == h, query, 0.0).astype(BF)
                g_rows[at, :] = jnp.where(lane_head == h, gout, 0.0).astype(BF)
                inner[h : h + 1, :] = jnp.sum(
                    inner_t[h * HEAD_DIM : (h + 1) * HEAD_DIM, :], axis=0, keepdims=True
                )
            grad_q[...] = jnp.zeros_like(grad_q)

            def tile(j, carry, masks):
                key_block, value_block = keys[j], values[j]
                if masks:
                    key_pos = j * blk + lax.broadcasted_iota(jnp.int32, (blk, blk), 0)
                    query_pos = i * blk + lax.broadcasted_iota(jnp.int32, (blk, blk), 1)
                    allowed = (key_pos <= query_pos) & (key_pos < live)
                probs, grads = [], []
                for h in range(heads):
                    s = mm(key_block, q_cols[h])
                    if masks:
                        s = jnp.where(allowed, s, NEG)
                    p = jnp.exp(s - lse_ref[i, h : h + 1, :])
                    d = p * (mm(value_block, g_cols[h]) - inner[h : h + 1, :])
                    probs.append(p.astype(BF))
                    d = d.astype(BF)
                    grads.append(d)
                    at = slice(h * HEAD_DIM, (h + 1) * HEAD_DIM)
                    grad_q[at, :] += mm(keys_t[j, at, :], d)
                grad_v[j] += mm(jnp.concatenate(probs, axis=1), g_rows[...])
                grad_k[j] += mm(jnp.concatenate(grads, axis=1), q_rows[...])
                return carry

            whole = jnp.minimum(i, lax.div(live, blk))
            lax.fori_loop(0, whole, lambda j, c: tile(j, c, False), 0)
            lax.fori_loop(whole, i + 1, lambda j, c: tile(j, c, True), 0)
            result_ref[rows_at, :width] = turned(
                jnp.transpose(grad_q[...]) * 0.125, cos_ref[rows_at, :], sin_ref[rows_at, :], True
            ).astype(BF)
            return carry

        lax.fori_loop(0, nb, per_block, 0)

        def drain(p, carry):
            rows_at = pl.ds(pl.multiple_of(order_ref[p] * blk, blk), blk)
            result_ref[rows_at, width : 2 * width] = turned(
                grad_k[p], cos_ref[rows_at, :], sin_ref[rows_at, :], True
            ).astype(BF)
            result_ref[rows_at, 2 * width :] = grad_v[p].astype(BF)
            return carry

        lax.fori_loop(0, nb, drain, 0)

    tiles = nb * (nb + 1) // 2 * heads
    vm = pl.BlockSpec(memory_space=pltpu.VMEM)
    sm = pl.BlockSpec(memory_space=pltpu.SMEM)
    return pl.pallas_call(
        body,
        in_specs=[sm, sm] + [vm] * 6,
        out_specs=vm,
        out_shape=jax.ShapeDtypeStruct((rows, 3 * width), BF),
        scratch_shapes=[
            pltpu.VMEM((nb, blk, width), BF),
            pltpu.VMEM((nb, width, blk), BF),
            pltpu.VMEM((nb, blk, width), BF),
            pltpu.VMEM((heads, width, blk), BF),
            pltpu.VMEM((heads * blk, width), BF),
            pltpu.VMEM((heads, width, blk), BF),
            pltpu.VMEM((heads * blk, width), BF),
            pltpu.VMEM((width, blk), F32),
            pltpu.VMEM((nb, blk, width), F32),
            pltpu.VMEM((nb, blk, width), F32),
            pltpu.VMEM((8, blk), F32),
        ],
        compiler_params=pltpu.CompilerParams(vmem_limit_bytes=40 << 20),
        cost_estimate=pl.CostEstimate(
            flops=tiles * 20 * blk * blk * width // 4,
            bytes_accessed=12 << 20,
            transcendentals=tiles * blk * blk,
        ),
        name="attention_back",
    )(order, length, qkv, grad_out, out, lse, cosine, sine_signed)


def gelu_both(u):
    scale = math.sqrt(2.0 / math.pi)
    inside = jnp.tanh(scale * (u + 0.044715 * u * u * u))
    value = 0.5 * u * (1.0 + inside)
    slope = 0.5 * (1.0 + inside) + 0.5 * u * (1.0 - inside * inside) * scale * (
        1.0 + 3.0 * 0.044715 * u * u
    )
    return value, slope


def per_device(n, hidden_in, cotangent, lengths, block_of, w_qkv, w_attn, w_up, w_down, norm_gains):
    own_rows, dim = hidden_in.shape[1:]
    rows = 4 * own_rows
    blk = own_rows // 2
    ff = w_up.shape[1]
    shard = dim // n
    ff_shard = ff // n
    ff_half = ff_shard // 2
    part = dim // 4
    extra = 16
    q = lax.axis_index("ctx")
    c = lax.rem(q, 2)
    length = lengths[0]

    groups = [lax.bitwise_xor(q, g) for g in range(4)]
    blocks = jnp.concatenate([lax.dynamic_slice_in_dim(block_of, g, 1, 0)[0] for g in groups])
    order = jnp.sum(
        jnp.where(
            blocks[None, :] == jnp.arange(8, dtype=jnp.int32)[:, None],
            jnp.arange(8, dtype=jnp.int32)[None, :],
            0,
        ),
        axis=1,
        dtype=jnp.int32,
    )
    offsets = jnp.arange(blk, dtype=jnp.int32)
    pos = (blocks[:, None] * blk + offsets[None, :]).reshape(-1)
    lane = jnp.arange(128, dtype=jnp.int32)
    half_dim = HEAD_DIM // 2
    inverse = jnp.exp((lane % half_dim).astype(F32) * (-2.0 * math.log(10000.0) / HEAD_DIM))
    angles = pos.astype(F32)[:, None] * inverse[None, :]
    cosine = jnp.cos(angles)
    sine_signed = jnp.sin(angles) * jnp.where(lane % HEAD_DIM < half_dim, -1.0, 1.0)[None, :]

    parts = [
        lax.dynamic_slice_in_dim(w_qkv, t * dim + q * part, part, 1) for t in range(3)
    ] + [lax.dynamic_slice_in_dim(w_attn, q * part, part, 1)]
    gain_rows = jnp.pad(norm_gains.T, ((0, extra - 4), (0, dim - shard)))
    bundle = jnp.concatenate([jnp.concatenate(parts, axis=1), gain_rows], axis=0)
    up_own = lax.dynamic_index_in_dim(
        w_up.reshape(shard, n, 2, ff_half), c, 2, keepdims=False
    ).reshape(shard, n * ff_half)
    down_own = lax.dynamic_slice_in_dim(w_down, c * ff_half, ff_half, 0)

    def store_bundle(target, owner, block):
        to_qkv, to_attn, to_gains = target
        return (
            lax.dynamic_update_slice(to_qkv, block[:shard, : 3 * part], (owner * shard, 0)),
            lax.dynamic_update_slice(to_attn, block[:shard, 3 * part :], (owner * shard, 0)),
            lax.dynamic_update_slice(to_gains, block[None, shard:, :shard], (owner, 0, 0)),
        )

    def store_rows(target, owner, block):
        return lax.dynamic_update_slice(target, block, (owner * block.shape[0], 0))

    hidden_b = hidden_in[0]
    hidden_x = swap(hidden_b, 2)
    hidden_c = swap(hidden_b, 1)
    hidden_d = swap(hidden_x, 1)
    qkv_w, attn_q, gains_n = ring_gather(
        bundle,
        n,
        False,
        store_bundle,
        (
            jnp.zeros((dim, 3 * part), BF),
            jnp.zeros((dim, part), BF),
            jnp.zeros((n, extra, shard), BF),
        ),
    )
    up_w = ring_gather(up_own, n, False, store_rows, jnp.zeros((dim, n * ff_half), BF))
    down_w = ring_gather(down_own, n, True, store_rows, jnp.zeros((n * ff_half, dim), BF))
    gains = jnp.transpose(gains_n[:, :4, :], (1, 0, 2)).reshape(4, dim).astype(F32)

    hidden_all = jnp.concatenate([hidden_b, hidden_c, hidden_x, hidden_d], axis=0)
    normed, qkv = project(hidden_all, qkv_w, gains[0:1], cosine, sine_signed)
    attn_x = swap(attn_q, 2)
    attn_pair = swap(jnp.stack([attn_q, attn_x]), 1)
    attn_parts = jnp.stack([attn_q, attn_pair[0], attn_x, attn_pair[1]])

    def in_order(stacked, axis):
        return jnp.concatenate(
            [
                lax.dynamic_index_in_dim(stacked, lax.bitwise_xor(q, b), 0, keepdims=False)
                for b in range(4)
            ],
            axis=axis,
        )

    attn_w = in_order(attn_parts, 1)
    att, lse = attention(order, length[None], qkv, blk)
    att_g = att.reshape(4, own_rows, part)
    attended = in_order(jnp.stack([att_g[0]] + [swap(att_g[g], g) for g in range(1, 4)]), 1)
    hidden = hidden_b.astype(F32)
    branch = mm(attended, attn_w)
    unit1, scale1 = normalize(branch)
    middle = hidden + unit1 * gains[1]
    unit2, scale2 = normalize(middle)
    normed_mid = (unit2 * gains[2]).astype(BF)
    normed_mid2 = jnp.concatenate([normed_mid, swap(normed_mid, 1)], axis=0)
    lifted = mm(normed_mid2, up_w)
    activated = gelu_both(lifted)[0].astype(BF)
    lowered = swap(mm(activated[own_rows:], down_w), 1) + mm(activated[:own_rows], down_w)
    unit3, scale3 = normalize(lowered)
    result = middle + unit3 * gains[3]

    live = (pos[:own_rows] < length).astype(F32)[:, None]
    upstream = cotangent[0].astype(F32) * live
    grad_lowered = norm_back(unit3, scale3, gains[3], upstream).astype(BF)
    grad_lowered2 = jnp.concatenate([grad_lowered, swap(grad_lowered, 1)], axis=0)
    grad_activated = mm_nt(grad_lowered2, down_w)
    grad_lifted = (grad_activated * gelu_both(lifted)[1]).astype(BF)
    down_g = mm_tn(activated, grad_lowered2).astype(BF)
    up_g = mm_tn(normed_mid2, grad_lifted).astype(BF)
    grad_normed_mid = swap(mm_nt(grad_lifted[own_rows:], up_w), 1) + mm_nt(
        grad_lifted[:own_rows], up_w
    )
    grad_middle = upstream + norm_back(unit2, scale2, gains[2], grad_normed_mid)
    grad_branch = norm_back(unit1, scale1, gains[1], grad_middle).astype(BF)
    grad_attended = mm_nt(grad_branch, attn_w).astype(BF)
    to_groups = [lax.dynamic_slice_in_dim(grad_attended, g * part, part, 1) for g in groups]
    grad_out = jnp.concatenate(
        [to_groups[0]] + [swap(to_groups[g], g) for g in range(1, 4)], axis=0
    )
    attn_g = mm_tn(attended, grad_branch).astype(BF)
    half_cols = dim // 2
    attn_half = lax.dynamic_slice_in_dim(attn_g, c * half_cols, half_cols, 1).astype(F32) + swap(
        lax.dynamic_slice_in_dim(attn_g, (1 - c) * half_cols, half_cols, 1), 1
    ).astype(F32)
    attn_half = attn_half.astype(BF)
    down_sum = ring_scatter(
        lambda s: lax.dynamic_slice_in_dim(down_g, s * ff_half, ff_half, 0), n, False
    )
    up_sum = ring_scatter(
        lambda s: jnp.concatenate(
            [
                lax.dynamic_slice_in_dim(up_g, s * shard, shard, 0),
                lax.dynamic_slice_in_dim(attn_half, s * shard, shard, 0),
            ],
            axis=1,
        ),
        n,
        True,
    )
    grad_mixed = attention_back(
        order, length[None], qkv, grad_out, att, lse, cosine, sine_signed, blk
    )
    qkv_g = mm_tn(normed, grad_mixed).astype(BF)
    partial = mm_nt(grad_mixed, qkv_w).astype(BF).reshape(4, own_rows, dim)
    came = swap(jnp.stack([partial[1], partial[3]]), 1).astype(F32)
    own_part = partial[0].astype(F32) + came[0]
    for_x = (partial[2].astype(F32) + came[1]).astype(BF)
    grad_normed = own_part + swap(for_x, 2).astype(F32)
    unit0, scale0 = normalize(hidden)
    input_grad = grad_middle + norm_back(unit0, scale0, gains[0], grad_normed)
    gains_g = jnp.stack(
        [
            jnp.sum(grad_normed * unit0, axis=0),
            jnp.sum(grad_middle * unit1, axis=0),
            jnp.sum(grad_normed_mid * unit2, axis=0),
            jnp.sum(upstream * unit3, axis=0),
        ]
    ).astype(BF)
    gains_p = jnp.pad(
        jnp.transpose(gains_g.reshape(4, n, shard), (1, 0, 2)),
        ((0, 0), (0, extra - 4), (0, 3 * part - shard)),
    )
    last = ring_scatter(
        lambda s: jnp.concatenate(
            [
                lax.dynamic_slice_in_dim(qkv_g, s * shard, shard, 0),
                lax.dynamic_index_in_dim(gains_p, s, 0, keepdims=False),
            ],
            axis=0,
        ),
        n,
        False,
    )

    def rounded(value):
        return lax.reduce_precision(value, 8, 7)

    def both_x(value):
        value = rounded(value)
        return value + swap(value.astype(BF), 2).astype(F32)

    down_x, up_x = both_x(down_sum), both_x(up_sum)
    down_both = jnp.stack([down_x, swap(down_x, 1)])
    up_both = jnp.stack([up_x, swap(up_x, 1)])

    def by_core(stacked):
        return [
            lax.dynamic_index_in_dim(stacked, lax.bitwise_xor(c, b), 0, keepdims=False)
            for b in range(2)
        ]

    down_out = jnp.concatenate(by_core(down_both), axis=0)
    up_two = by_core(up_both)
    mlp_width = n * ff_half
    up_out = jnp.stack(
        [v[:, :mlp_width].reshape(shard, n, ff_half) for v in up_two], axis=2
    ).reshape(shard, ff)
    attn_out = jnp.concatenate([v[:, mlp_width:] for v in up_two], axis=1)
    last = rounded(last)
    last_b = last.astype(BF)
    last_x = swap(last_b, 2)
    last_pair = swap(jnp.stack([last_b, last_x]), 1)
    stacked = jnp.stack([last_b, last_pair[0], last_x, last_pair[1]])
    quarters = [
        lax.dynamic_index_in_dim(stacked, lax.bitwise_xor(q, b), 0, keepdims=False).astype(F32)
        for b in range(4)
    ]
    qkv_out = jnp.concatenate(
        [quarters[b][:shard, t * part : (t + 1) * part] for t in range(3) for b in range(4)],
        axis=1,
    )
    gains_out = (
        quarters[0][shard : shard + 4, :shard]
        + quarters[1][shard : shard + 4, :shard]
        + quarters[2][shard : shard + 4, :shard]
        + quarters[3][shard : shard + 4, :shard]
    ).T
    return (
        result.astype(BF)[None],
        input_grad[None],
        qkv_out,
        attn_out,
        up_out,
        down_out,
        gains_out,
    )


def solution(mesh):
    n = mesh.shape["fsdp"]

    def step(*args):
        return per_device(n, *args)

    rows = P("fsdp", "ctx", None)
    weight = P("fsdp", None)
    return jax.shard_map(
        step,
        mesh=mesh,
        in_specs=(rows, rows, P("fsdp"), P()) + (weight,) * 5,
        out_specs=(rows, rows) + (weight,) * 5,
        check_vma=False,
    )
```

time: 2390 us -> 488 us (0.20)
  waiting for transfers between devices: 1450 us -> 165 us
  local copies, waits for them, and re-layouts: 487 us -> 53.8 us
  matrix products: 312 us -> 60.3 us
  Pallas kernels: 0 us -> 88.9 us
  starting transfers between devices: 1.14 us -> 62.1 us
  blocking collectives: 28.9 us -> 0 us
  other arithmetic: 71.7 us -> 44.8 us
    reduce_scatter x6 -> x0, waiting for transfers between devices: 946 us -> none  [the longest x1 287 us: per_device(): lax.psum_scatter(grad_down, 'fsdp', scatter_dimension=0, tiled=True)]
    dynamic_update_slice x32 -> x39, local copies, waits for them, and re-layouts: 405 us -> 30.1 us  [the longest x16 19.9 us: store_rows(): return lax.dynamic_update_slice(target, block, (owner * block.shape[0], 0))]
    all_gather x6 -> x0, waiting for transfers between devices: 328 us -> none  [the longest x1 113 us: gather_weights(): lax.all_gather(w_down, 'fsdp', axis=0, tiled=True)]
    dot_general x84 -> x13, matrix products: 312 us -> 60.3 us  [the longest x5 22 us: mm_nt(): lax.dot_general(left, right, (((1,), (1,)), ((), ())), preferred_element_...]
    ppermute x0 -> x66, waiting for transfers between devices: none -> 165 us  [the longest x12 56.5 us: ring_scatter(): one = lax.ppermute(one, 'fsdp', ahead)]
    psum x1 -> x0, waiting for transfers between devices: 115 us -> none  [per_device(): lax.psum((summed[0], summed[1], summed[2], summed[3], summed[4]), 'ctx')]
    pallas_call x0 -> x3, Pallas kernels: none -> 88.9 us  [the longest x1 56.4 us: attention_back(): pl.pallas_call(body, in_specs=[sm, sm] + [vm] * 6, out_specs=vm, out_shap...]
    unnamed x15 -> x0, waiting for transfers between devices: 62.4 us -> none
  transfers between devices with their start and end apart: 14 -> 66, of which waited for: 12 -> 29; matrix products, arithmetic and copies ran while one was open for 8% -> 24% of each run, Pallas kernels for 0% -> 19%
where the time goes in v1:
time: 488 us; the launch traced here: 479 us
  waiting for transfers between devices  165 us (34%)
  Pallas kernels  88.9 us (18%)
  starting transfers between devices  62.1 us (13%)
  matrix products  60.3 us (12%)
  local copies, waits for them, and re-layouts  53.8 us (11%)
  other arithmetic  44.8 us (9%)
    ppermute x12, waiting for transfers between devices, ring_scatter(): one = lax.ppermute(one, 'fsdp', ahead)  56.5 us
    pallas_call x1, Pallas kernels, attention_back(): pl.pallas_call(body, in_specs=[sm, sm] + [vm] * 6, out_specs=vm, out_shap...  56.4 us
    ppermute x12, waiting for transfers between devices, ring_gather(): one = lax.ppermute(one, 'fsdp', ahead)  44.5 us
    ppermute x24, waiting for transfers between devices, swap(): return lax.ppermute(value, 'ctx', [(i, i ^ bit) for i in range(4)])  34.6 us
    pallas_call x1, Pallas kernels, attention(): pl.pallas_call(body, in_specs=[sm, sm, vm], out_specs=[vm, vm], out_shape...  25.6 us
    dot_general x5, matrix products, mm_nt(): lax.dot_general(left, right, (((1,), (1,)), ((), ())), preferred_element_...  22 us
    dot_general x4, matrix products, mm(): return jnp.dot(left, right, preferred_element_type=F32)  21.1 us
    dynamic_update_slice x16, local copies, waits for them, and re-layouts, store_rows(): return lax.dynamic_update_slice(target, block, (owner * block.shape[0], 0))  19.9 us
  transfers between devices with their start and end apart: 66, of which 29 were waited for; matrix products, arithmetic and copies ran while one was open for 24% of the time, Pallas kernels for 19%

profile of v1, /device:TPU:0, one launch (start us, length us, event | category | flops | bytes accessed | tf_op | source)
XLA Modules:
  0.0 478.8 jit_solution(3215150093350518789)
XLA Ops:
  17.7 5.0 %fusion.47 = (f32[2048,128]{1,0:T(8,128)S(1)}, f32[2048,128]{1,0:T(8,128)}) fusion(f32[128]{0:T(128)S(1)} %get-tuple-element.131, f32[128]{0:T(128)S(1)} %get-tuple-element.132, f32[2048]{0:T(1024)S(1)} %bitcast.204), kind=kLoop, calls=%fused_computation.104 | loop fusion | flops 524288 | bytes 2106368 | tf_op jit(solution)/shard_map/mul | solution.py:435
  24.6 13.9 %collective-permute-done.3 = bf16[144,1024]{1,0:T(8,128)(2,1)} collective-permute-done((bf16[144,1024]{1,0:T(8,128)(2,1)S(1)}, bf16[144,1024]{1,0:T(8,128)(2,1)}, u32[]{:S(2)}, u32[]{:S(2)}) %collective-permute-start.3) | collective-permute-done | bytes 294944 | tf_op jit(solution)/shard_map/ppermute | solution.py:58
  67.4 12.8 %collective-permute-done.7 = bf16[144,1024]{1,0:T(8,128)(2,1)S(1)} collective-permute-done((bf16[144,1024]{1,0:T(8,128)(2,1)}, bf16[144,1024]{1,0:T(8,128)(2,1)S(1)}, u32[]{:S(2)}, u32[]{:S(2)}) %collective-permute-start.7) | collective-permute-done | bytes 294944 | tf_op jit(solution)/shard_map/ppermute | solution.py:58
  81.9 6.3 %collective-permute-done.8 = bf16[144,1024]{1,0:T(8,128)(2,1)S(1)} collective-permute-done((bf16[144,1024]{1,0:T(8,128)(2,1)}, bf16[144,1024]{1,0:T(8,128)(2,1)S(1)}, u32[]{:S(2)}, u32[]{:S(2)}) %collective-permute-start.8) | collective-permute-done | bytes 294944 | tf_op jit(solution)/shard_map/ppermute | solution.py:60
  94.1 9.2 %collective-permute-done.18 = bf16[128,2048]{0,1:T(8,128)(2,1)} collective-permute-done((bf16[128,2048]{0,1:T(8,128)(2,1)}, bf16[128,2048]{0,1:T(8,128)(2,1)}, u32[]{:S(2)}, u32[]{:S(2)}) %collective-permute-start.18) | collective-permute-done | bytes 524320 | tf_op jit(solution)/shard_map/ppermute | solution.py:58
  110.5 12.3 %collective-permute-done.13 = bf16[1024,256]{1,0:T(8,128)(2,1)} collective-permute-done((bf16[1024,256]{1,0:T(8,128)(2,1)S(1)}, bf16[1024,256]{1,0:T(8,128)(2,1)}, u32[]{:S(2)}, u32[]{:S(2)}) %collective-permute-start.13) | collective-permute-done | bytes 524320 | tf_op jit(solution)/shard_map/ppermute | solution.py:30
  128.5 6.8 %project.1 = (bf16[2048,1024]{1,0:T(8,128)(2,1)S(1)}, bf16[2048,768]{1,0:T(8,128)(2,1)S(1)}) custom-call(bf16[2048,1024]{1,0:T(8,128)(2,1)S(1)} %pad_maximum_fusion.hidden_ref, bf16[1024,768]{1,0:T(8,128)(2,1)S(1)} %slice_dynamic-update-slice_fusion.weight_ref, f32[1,1024]{1,0:T(1,128)S(1)} %bitcast.178, f32[2048,128]{1,0:T(8,128)S(1)} %copy-done.2, ...), custom_call_target="tpu_custom_call" | custom-call | flops 3221225472 | bytes 12582912 | tf_op jit(solution)/shard_map/project/pallas_call | solution.py:145
  135.4 25.6 %attention.1 = (bf16[2048,256]{1,0:T(8,128)(2,1)S(1)}, f32[8,8,256]{2,1,0:T(8,128)S(1)}) custom-call(s32[8]{0:T(128)S(1)} %select_reduce_fusion.order_ref, s32[1]{0:T(128)} %copy.145.length_ref, bf16[2048,768]{1,0:T(8,128)(2,1)S(1)} %get-tuple-element.11.qkv_ref), custom_call_target="tpu_custom_call" | custom-call | flops 4831838208 | bytes 5242880 | tf_op jit(solution)/shard_map/attention/pallas_call | solution.py:252
  187.0 8.2 %collective-permute-done.29 = bf16[256,1024]{1,0:T(8,128)(2,1)S(1)} collective-permute-done((bf16[256,1024]{1,0:T(8,128)(2,1)S(1)}, bf16[256,1024]{1,0:T(8,128)(2,1)S(1)}, u32[]{:S(2)}, u32[]{:S(2)}) %collective-permute-start.29) | collective-permute-done | bytes 524320 | tf_op jit(solution)/shard_map/ppermute | solution.py:58
  196.2 9.1 %multiply_convert_fusion = (bf16[1024,2048]{1,0:T(8,128)(2,1)S(1)}, f32[1024,2048]{1,0:T(8,128)}) fusion(bf16[1024,2048]{0,1:T(8,128)(2,1)S(1)} %constant_dynamic-update-slice_fusion.8, bf16[512,1024]{1,0:T(8,128)(2,1)S(1)} %collective-permute-done.15, bf16[512,1024]{1,0:T(8,128)(2,1)S(1)} %multiply_convert_fusion.2), kind=kOutput, calls=%fused_computation.9 | convolution fusion | flops 4318035968 | bytes 18874368 | tf_op jit(solution)/shard_map/dot_general | solution.py:18
  205.3 6.1 %fusion.29 = f32[512,1024]{1,0:T(8,128)S(1)} fusion(bf16[2048,1024]{1,0:T(8,128)(2,1)} %constant_dynamic-update-slice_fusion, bf16[1024,2048]{1,0:T(8,128)(2,1)S(1)} %get-tuple-element.129), kind=kOutput, calls=%fused_computation.49 | convolution fusion | flops 2147483648 | bytes 8388608 | tf_op jit(solution)/shard_map/dot_general | solution.py:18
  224.2 7.4 %convolution_convert_fusion.1 = bf16[2048,1024]{1,0:T(8,128)(2,1)S(1)} fusion(bf16[1024,2048]{1,0:T(8,128)(2,1)} %copy-done.48, bf16[512,1024]{1,0:T(8,128)(2,1)} %collective-permute-done.31, bf16[512,1024]{1,0:T(8,128)(2,1)} %get-tuple-element.62), kind=kOutput, calls=%fused_computation.12 | convolution fusion | flops 4301258752 | bytes 10485760 | tf_op jit(solution)/shard_map/dot_general | solution.py:22
  232.1 12.1 %fusion.6 = bf16[1024,2048]{1,0:T(8,128)(2,1)S(1)} fusion(f32[1024,2048]{1,0:T(8,128)} %get-tuple-element.130, bf16[2048,1024]{1,0:T(8,128)(2,1)} %constant_dynamic-update-slice_fusion, bf16[512,1024]{1,0:T(8,128)(2,1)} %collective-permute-done.31, bf16[512,1024]{1,0:T(8,128)(2,1)} %get-tuple-element.62), kind=kOutput, calls=%fused_computation.8 | convolution fusion | flops 4339007488 | bytes 18874368 | tf_op jit(solution)/shard_map/dot_general | solution.py:26
  249.0 5.0 %convolution_convert_fusion.2 = bf16[1024,2048]{1,0:T(8,128)(2,1)S(1)} fusion(bf16[1024,2048]{1,0:T(8,128)(2,1)S(1)} %fusion.6, bf16[512,1024]{1,0:T(8,128)(2,1)S(1)} %copy-done.47, bf16[512,1024]{1,0:T(8,128)(2,1)S(1)} %copy-done.21), kind=kOutput, calls=%fused_computation.13 | convolution fusion | flops 4301258752 | bytes 10485760 | tf_op jit(solution)/shard_map/dot_general | solution.py:22
  255.3 5.7 %collective-permute-done.61 = bf16[256,1024]{1,0:T(8,128)(2,1)S(1)} collective-permute-done((bf16[256,1024]{1,0:T(8,128)(2,1)S(1)}, bf16[256,1024]{1,0:T(8,128)(2,1)S(1)}, u32[]{:S(2)}, u32[]{:S(2)}) %collective-permute-start.61) | collective-permute-done | bytes 524320 | tf_op jit(solution)/shard_map/ppermute | solution.py:82
  267.4 8.8 %collective-permute-done.59 = bf16[256,1024]{1,0:T(8,128)(2,1)S(1)} collective-permute-done((bf16[256,1024]{1,0:T(8,128)(2,1)S(1)}, bf16[256,1024]{1,0:T(8,128)(2,1)S(1)}, u32[]{:S(2)}, u32[]{:S(2)}) %collective-permute-start.59) | collective-permute-done | bytes 524320 | tf_op jit(solution)/shard_map/ppermute | solution.py:80
  294.2 4.7 collective-permute-done.34
  299.0 56.4 %attention_back.1 = bf16[2048,768]{1,0:T(8,128)(2,1)S(1)} custom-call(s32[8]{0:T(128)S(1)} %select_reduce_fusion.order_ref, s32[1]{0:T(128)} %copy.145.length_ref, bf16[2048,768]{1,0:T(8,128)(2,1)S(1)} %copy-done.7, bf16[2048,256]{1,0:T(8,128)(2,1)S(1)} %pad_maximum_fusion.15.gout_ref, bf16[2048,256]{1,0:T(8,128)(2,1)S(1)} %get-tuple-element.12.att_ref, ...), custom_call_target="tpu_custom_call" | custom-call | flops 12079595520 | bytes 12582912 | tf_op jit(solution)/shard_map/attention_back/pallas_call | solution.py:365
  374.1 12.5 %collective-permute-done.48 = bf16[128,2560]{1,0:T(8,128)(2,1)S(1)} collective-permute-done((bf16[128,2560]{1,0:T(8,128)(2,1)S(1)}, bf16[128,2560]{1,0:T(8,128)(2,1)S(1)}, u32[]{:S(2)}, u32[]{:S(2)}) %collective-permute-start.48) | collective-permute-done | bytes 655392 | tf_op jit(solution)/shard_map/ppermute | solution.py:80
  390.9 11.7 %collective-permute-done.49 = bf16[128,2560]{1,0:T(8,128)(2,1)S(1)} collective-permute-done((bf16[128,2560]{1,0:T(8,128)(2,1)S(1)}, bf16[128,2560]{1,0:T(8,128)(2,1)S(1)}, u32[]{:S(2)}, u32[]{:S(2)}) %collective-permute-start.49) | collective-permute-done | bytes 655392 | tf_op jit(solution)/shard_map/ppermute | solution.py:80
  405.1 12.7 %collective-permute-done.50 = bf16[128,2560]{1,0:T(8,128)(2,1)S(1)} collective-permute-done((bf16[128,2560]{1,0:T(8,128)(2,1)S(1)}, bf16[128,2560]{1,0:T(8,128)(2,1)S(1)}, u32[]{:S(2)}, u32[]{:S(2)}) %collective-permute-start.50) | collective-permute-done | bytes 655392 | tf_op jit(solution)/shard_map/ppermute | solution.py:80
  424.6 6.9 %collective-permute-done.38 = bf16[144,768]{1,0:T(8,128)(2,1)S(1)} collective-permute-done((bf16[144,768]{1,0:T(8,128)(2,1)S(1)}, bf16[144,768]{1,0:T(8,128)(2,1)S(1)}, u32[]{:S(2)}, u32[]{:S(2)}) %collective-permute-start.38) | collective-permute-done | bytes 221216 | tf_op jit(solution)/shard_map/ppermute | solution.py:80
  431.9 5.6 %collective-permute-done.42 = bf16[144,768]{1,0:T(8,128)(2,1)S(1)} collective-permute-done((bf16[144,768]{1,0:T(8,128)(2,1)S(1)}, bf16[144,768]{1,0:T(8,128)(2,1)S(1)}, u32[]{:S(2)}, u32[]{:S(2)}) %collective-permute-start.42) | collective-permute-done | bytes 221216 | tf_op jit(solution)/shard_map/ppermute | solution.py:82
  439.7 5.8 %collective-permute-done.43 = bf16[144,768]{1,0:T(8,128)(2,1)S(1)} collective-permute-done((bf16[144,768]{1,0:T(8,128)(2,1)S(1)}, bf16[144,768]{1,0:T(8,128)(2,1)S(1)}, u32[]{:S(2)}, u32[]{:S(2)}) %collective-permute-start.43) | collective-permute-done | bytes 221216 | tf_op jit(solution)/shard_map/ppermute | solution.py:82
  (410 shorter events, 204.8 us)
Async XLA Ops:
  4.3 44.1 %collective-permute-start.23 = (bf16[256,1024]{1,0:T(8,128)(2,1)}, bf16[256,1024]{1,0:T(8,128)(2,1)}, u32[]{:S(2)}, u32[]{:S(2)}) collective-permute-start(bf16[256,1024]{1,0:T(8,128)(2,1)} %get-tuple-element.39), channel_id=1, source_target_pairs={{2,0},{4,2},{6,4},{7,6},{5,7},{3,5},{1,3},{0,1},{10,8},{12,10},{14... | collective-permute-start | bytes 1572872 | tf_op jit(solution)/shard_map/ppermute | solution.py:58
  7.3 45.6 %collective-permute-start.24 = (bf16[256,1024]{1,0:T(8,128)(2,1)}, bf16[256,1024]{1,0:T(8,128)(2,1)}, u32[]{:S(2)}, u32[]{:S(2)}) collective-permute-start(bf16[256,1024]{1,0:T(8,128)(2,1)} %get-tuple-element.39), channel_id=1, source_target_pairs={{0,2},{2,4},{4,6},{6,7},{7,5},{5,3},{3,1},{1,0},{8,10},{10,12},{12... | collective-permute-start | bytes 1572872 | tf_op jit(solution)/shard_map/ppermute | solution.py:60
  8.8 41.6 %collective-permute-start.16 = (bf16[128,2048]{0,1:T(8,128)(2,1)}, bf16[128,2048]{0,1:T(8,128)(2,1)}, u32[]{:S(2)}, u32[]{:S(2)}) collective-permute-start(bf16[128,2048]{0,1:T(8,128)(2,1)} %bitcast.29), channel_id=1, source_target_pairs={{0,2},{2,4},{4,6},{6,7},{7,5},{5,3},{3,1},{1,0},{8,10},{10,12},{12... | collective-permute-start | bytes 1572872 | tf_op jit(solution)/shard_map/ppermute | solution.py:58
  10.9 45.4 %collective-permute-start.17 = (bf16[128,2048]{0,1:T(8,128)(2,1)}, bf16[128,2048]{0,1:T(8,128)(2,1)}, u32[]{:S(2)}, u32[]{:S(2)}) collective-permute-start(bf16[128,2048]{0,1:T(8,128)(2,1)} %bitcast.29), channel_id=1, source_target_pairs={{2,0},{4,2},{6,4},{7,6},{5,7},{3,5},{1,3},{0,1},{10,8},{12,10},{14... | collective-permute-start | bytes 1572872 | tf_op jit(solution)/shard_map/ppermute | solution.py:60
  12.7 25.8 %collective-permute-start.3 = (bf16[144,1024]{1,0:T(8,128)(2,1)S(1)}, bf16[144,1024]{1,0:T(8,128)(2,1)}, u32[]{:S(2)}, u32[]{:S(2)}) collective-permute-start(bf16[144,1024]{1,0:T(8,128)(2,1)S(1)} %pad_maximum_fusion.24), channel_id=1, source_target_pairs={{0,2},{2,4},{4,6},{6,7},{7,5},{5,3},{3,1},{1,0},{8,10},{10,12},{12... | collective-permute-start | bytes 884744 | tf_op jit(solution)/shard_map/ppermute | solution.py:58
  46.1 58.9 %collective-permute-start.1 = (bf16[512,1024]{1,0:T(8,128)(2,1)}, bf16[512,1024]{1,0:T(8,128)(2,1)}, u32[]{:S(2)}, u32[]{:S(2)}) collective-permute-start(bf16[512,1024]{1,0:T(8,128)(2,1)} %bitcast), channel_id=1, source_target_pairs={{0,16},{8,24},{16,0},{24,8},{1,17},{9,25},{17,1},{25,9},{2,18},{10... | collective-permute-start | bytes 3145736 | tf_op jit(solution)/shard_map/ppermute | solution.py:30
  48.5 77.1 %collective-permute-start = (bf16[512,1024]{1,0:T(8,128)(2,1)}, bf16[512,1024]{1,0:T(8,128)(2,1)}, u32[]{:S(2)}, u32[]{:S(2)}) collective-permute-start(bf16[512,1024]{1,0:T(8,128)(2,1)} %bitcast), channel_id=1, source_target_pairs={{0,8},{8,0},{16,24},{24,16},{1,9},{9,1},{17,25},{25,17},{2,10},{10... | collective-permute-start | bytes 3145736 | tf_op jit(solution)/shard_map/ppermute | solution.py:30
  56.2 34.6 %collective-permute-start.25 = (bf16[256,1024]{1,0:T(8,128)(2,1)}, bf16[256,1024]{1,0:T(8,128)(2,1)}, u32[]{:S(2)}, u32[]{:S(2)}) collective-permute-start(bf16[256,1024]{1,0:T(8,128)(2,1)} %collective-permute-done.23), channel_id=1, source_target_pairs={{2,0},{4,2},{6,4},{7,6},{5,7},{3,5},{1,3},{0,1},{10,8},{12,10},{14... | collective-permute-start | bytes 1572872 | tf_op jit(solution)/shard_map/ppermute | solution.py:58
  60.1 101.0 %collective-permute-start.26 = (bf16[256,1024]{1,0:T(8,128)(2,1)}, bf16[256,1024]{1,0:T(8,128)(2,1)}, u32[]{:S(2)}, u32[]{:S(2)}) collective-permute-start(bf16[256,1024]{1,0:T(8,128)(2,1)} %collective-permute-done.24), channel_id=1, source_target_pairs={{0,2},{2,4},{4,6},{6,7},{7,5},{5,3},{3,1},{1,0},{8,10},{10,12},{12... | collective-permute-start | bytes 1572872 | tf_op jit(solution)/shard_map/ppermute | solution.py:60
  103.3 58.5 %collective-permute-start.19 = (bf16[128,2048]{0,1:T(8,128)(2,1)}, bf16[128,2048]{0,1:T(8,128)(2,1)}, u32[]{:S(2)}, u32[]{:S(2)}) collective-permute-start(bf16[128,2048]{0,1:T(8,128)(2,1)} %collective-permute-done.17), channel_id=1, source_target_pairs={{2,0},{4,2},{6,4},{7,6},{5,7},{3,5},{1,3},{0,1},{10,8},{12,10},{14... | collective-permute-start | bytes 1572872 | tf_op jit(solution)/shard_map/ppermute | solution.py:60
  104.9 21.1 %collective-permute-start.2 = (bf16[512,1024]{1,0:T(8,128)(2,1)}, bf16[512,1024]{1,0:T(8,128)(2,1)}, u32[]{:S(2)}, u32[]{:S(2)}) collective-permute-start(bf16[512,1024]{1,0:T(8,128)(2,1)} %collective-permute-done.1), channel_id=1, source_target_pairs={{0,8},{8,0},{16,24},{24,16},{1,9},{9,1},{17,25},{25,17},{2,10},{10... | collective-permute-start | bytes 3145736 | tf_op jit(solution)/shard_map/ppermute | solution.py:30
  122.8 40.5 %collective-permute-start.27 = (bf16[256,1024]{1,0:T(8,128)(2,1)}, bf16[256,1024]{1,0:T(8,128)(2,1)S(1)}, u32[]{:S(2)}, u32[]{:S(2)}) collective-permute-start(bf16[256,1024]{1,0:T(8,128)(2,1)} %collective-permute-done.25), channel_id=1, source_target_pairs={{2,0},{4,2},{6,4},{7,6},{5,7},{3,5},{1,3},{0,1},{10,8},{12,10},{14... | collective-permute-start | bytes 1572872 | tf_op jit(solution)/shard_map/ppermute | solution.py:58
  125.6 40.9 %collective-permute-start.20 = (bf16[128,2048]{0,1:T(8,128)(2,1)}, bf16[128,2048]{0,1:T(8,128)(2,1)S(1)}, u32[]{:S(2)}, u32[]{:S(2)}) collective-permute-start(bf16[128,2048]{0,1:T(8,128)(2,1)} %collective-permute-done.18), channel_id=1, source_target_pairs={{0,2},{2,4},{4,6},{6,7},{7,5},{5,3},{3,1},{1,0},{8,10},{10,12},{12... | collective-permute-start | bytes 1572872 | tf_op jit(solution)/shard_map/ppermute | solution.py:58
  126.1 51.9 %collective-permute-start.14 = (bf16[2,1024,256]{2,1,0:T(8,128)(2,1)S(1)}, bf16[2,1024,256]{2,1,0:T(8,128)(2,1)S(1)}, u32[]{:S(2)}, u32[]{:S(2)}) collective-permute-start(bf16[2,1024,256]{2,1,0:T(8,128)(2,1)S(1)} %pad_maximum_fusion.14), channel_id=1, source_target_pairs={{0,8},{8,0},{16,24},{24,16},{1,9},{9,1},{17,25},{25,17},{2,10},{10... | collective-permute-start | bytes 3145736 | tf_op jit(solution)/shard_map/ppermute | solution.py:30
  166.5 19.5 %collective-permute-start.28 = (bf16[256,1024]{1,0:T(8,128)(2,1)}, bf16[256,1024]{1,0:T(8,128)(2,1)S(1)}, u32[]{:S(2)}, u32[]{:S(2)}) collective-permute-start(bf16[256,1024]{1,0:T(8,128)(2,1)} %collective-permute-done.26), channel_id=1, source_target_pairs={{0,2},{2,4},{4,6},{6,7},{7,5},{5,3},{3,1},{1,0},{8,10},{10,12},{12... | collective-permute-start | bytes 1572872 | tf_op jit(solution)/shard_map/ppermute | solution.py:60
  175.4 19.7 %collective-permute-start.29 = (bf16[256,1024]{1,0:T(8,128)(2,1)S(1)}, bf16[256,1024]{1,0:T(8,128)(2,1)S(1)}, u32[]{:S(2)}, u32[]{:S(2)}) collective-permute-start(bf16[256,1024]{1,0:T(8,128)(2,1)S(1)} %collective-permute-done.27), channel_id=1, source_target_pairs={{2,0},{4,2},{6,4},{7,6},{5,7},{3,5},{1,3},{0,1},{10,8},{12,10},{14... | collective-permute-start | bytes 1572872 | tf_op jit(solution)/shard_map/ppermute | solution.py:58
  177.0 19.0 %collective-permute-start.22 = (bf16[128,2048]{0,1:T(8,128)(2,1)S(1)}, bf16[128,2048]{0,1:T(8,128)(2,1)S(1)}, u32[]{:S(2)}, u32[]{:S(2)}) collective-permute-start(bf16[128,2048]{0,1:T(8,128)(2,1)S(1)} %collective-permute-done.20), channel_id=1, source_target_pairs={{0,2},{2,4},{4,6},{6,7},{7,5},{5,3},{3,1},{1,0},{8,10},{10,12},{12... | collective-permute-start | bytes 1572872 | tf_op jit(solution)/shard_map/ppermute | solution.py:58
  246.6 32.3 %collective-permute-start.32 = (f32[512,1024]{1,0:T(8,128)S(1)}, f32[512,1024]{1,0:T(8,128)S(1)}, u32[]{:S(2)}, u32[]{:S(2)}) collective-permute-start(f32[512,1024]{1,0:T(8,128)S(1)} %fusion.25), channel_id=1, source_target_pairs={{0,8},{8,0},{16,24},{24,16},{1,9},{9,1},{17,25},{25,17},{2,10},{10... | collective-permute-start | bytes 6291464 | tf_op jit(solution)/shard_map/ppermute | solution.py:30
  289.9 78.2 %collective-permute-start.47 = (bf16[1024,512]{1,0:T(8,128)(2,1)}, bf16[1024,512]{1,0:T(8,128)(2,1)}, u32[]{:S(2)}, u32[]{:S(2)}) collective-permute-start(bf16[1024,512]{1,0:T(8,128)(2,1)} %constant_dynamic-slice_fusion.17), channel_id=1, source_target_pairs={{0,8},{8,0},{16,24},{24,16},{1,9},{9,1},{17,25},{25,17},{2,10},{10... | collective-permute-start | bytes 3145736 | tf_op jit(solution)/shard_map/ppermute | solution.py:30
  291.3 74.1 %collective-permute-start.64 = (bf16[256,1024]{1,0:T(8,128)(2,1)}, bf16[256,1024]{1,0:T(8,128)(2,1)}, u32[]{:S(2)}, u32[]{:S(2)}) collective-permute-start(bf16[256,1024]{1,0:T(8,128)(2,1)} %fusion.54), channel_id=1, source_target_pairs={{0,16},{8,24},{16,0},{24,8},{1,17},{9,25},{17,1},{25,9},{2,18},{10... | collective-permute-start | bytes 1572872 | tf_op jit(solution)/shard_map/ppermute | solution.py:30
  359.8 29.2 %collective-permute-start.36 = (bf16[2,512,1024]{2,1,0:T(8,128)(2,1)S(1)}, bf16[2,512,1024]{2,1,0:T(8,128)(2,1)S(1)}, u32[]{:S(2)}, u32[]{:S(2)}) collective-permute-start(bf16[2,512,1024]{2,1,0:T(8,128)(2,1)S(1)} %pad_maximum_fusion.5), channel_id=1, source_target_pairs={{0,8},{8,0},{16,24},{24,16},{1,9},{9,1},{17,25},{25,17},{2,10},{10... | collective-permute-start | bytes 6291464 | tf_op jit(solution)/shard_map/ppermute | solution.py:30
  389.9 29.7 %collective-permute-start.37 = (bf16[512,1024]{1,0:T(8,128)(2,1)S(1)}, bf16[512,1024]{1,0:T(8,128)(2,1)S(1)}, u32[]{:S(2)}, u32[]{:S(2)}) collective-permute-start(bf16[512,1024]{1,0:T(8,128)(2,1)S(1)} %fusion.20), channel_id=1, source_target_pairs={{0,16},{8,24},{16,0},{24,8},{1,17},{9,25},{17,1},{25,9},{2,18},{10... | collective-permute-start | bytes 3145736 | tf_op jit(solution)/shard_map/ppermute | solution.py:30
  404.6 43.5 %collective-permute-start.54 = (bf16[128,2560]{1,0:T(8,128)(2,1)S(1)}, bf16[128,2560]{1,0:T(8,128)(2,1)S(1)}, u32[]{:S(2)}, u32[]{:S(2)}) collective-permute-start(bf16[128,2560]{1,0:T(8,128)(2,1)S(1)} %add_convert_fusion.2), channel_id=1, source_target_pairs={{0,2},{2,4},{4,6},{6,7},{7,5},{5,3},{3,1},{1,0},{8,10},{10,12},{12... | collective-permute-start | bytes 1966088 | tf_op jit(solution)/shard_map/ppermute | solution.py:82
  417.9 30.2 %collective-permute-start.51 = (bf16[128,2560]{1,0:T(8,128)(2,1)S(1)}, bf16[128,2560]{1,0:T(8,128)(2,1)S(1)}, u32[]{:S(2)}, u32[]{:S(2)}) collective-permute-start(bf16[128,2560]{1,0:T(8,128)(2,1)S(1)} %add_convert_fusion.4), channel_id=1, source_target_pairs={{2,0},{4,2},{6,4},{7,6},{5,7},{3,5},{1,3},{0,1},{10,8},{12,10},{14... | collective-permute-start | bytes 1966088 | tf_op jit(solution)/shard_map/ppermute | solution.py:80
  (91 other events, 931.8 us)

commit v2 on v1

v2 whole, which is shorter than its diff:
```python
import math

import jax
import jax.numpy as jnp
from jax import lax
from jax.experimental import pallas as pl
from jax.experimental.pallas import tpu as pltpu
from jax.sharding import PartitionSpec as P

HEAD_DIM = 64
PAIR = 2 * HEAD_DIM
EXTRA = 16
BF = jnp.bfloat16
F32 = jnp.float32
NEG = -1e30
EPS = 1e-05
VM = pl.BlockSpec(memory_space=pltpu.VMEM)
SM = pl.BlockSpec(memory_space=pltpu.SMEM)


def mm(left, right):
    return jnp.dot(left, right, preferred_element_type=F32)


def mm_tn(left, right):
    return lax.dot_general(left, right, (((0,), (0,)), ((), ())), preferred_element_type=F32)


def mm_nt(left, right):
    return lax.dot_general(left, right, (((1,), (1,)), ((), ())), preferred_element_type=F32)


def swap(value, bit):
    return lax.ppermute(value, "ctx", [(i, i ^ bit) for i in range(4)])


def blank(shape, dtype):
    return pl.pallas_call(
        lambda out_ref: None,
        out_specs=pl.BlockSpec(memory_space=pl.ANY),
        out_shape=jax.ShapeDtypeStruct(shape, dtype),
        name="blank",
    )()


def ring_pairs(n):
    order = list(range(0, n, 2)) + list(range(n - 1, 0, -2))
    ahead = [(order[i], order[(i + 1) % n]) for i in range(n)]
    return ahead, [(b, a) for a, b in ahead]


def ring_owner(place, n):
    place = lax.rem(place + 2 * n, n)
    return jnp.where(place < n // 2, 2 * place, 2 * (n - place) - 1)


def ring_place(me, n):
    return jnp.where(lax.rem(me, 2) == 0, lax.div(me, 2), n - 1 - lax.div(me, 2))


def after(value, *others):
    return lax.optimization_barrier((value,) + others)[0] if others else value


class Gather:
    def __init__(self, block, n, flip, store, target):
        self.ahead, self.back = ring_pairs(n)
        self.sign = -1
        if flip:
            self.ahead, self.back, self.sign = self.back, self.ahead, 1
        me = lax.axis_index("fsdp")
        self.n, self.place, self.count = n, ring_place(me, n), 0
        self.store, self.one, self.two = store, block, block
        self.target = store(target, me, block)

    def step(self, *others):
        if self.count == self.n // 2:
            return
        self.count += 1
        n, hops = self.n, self.sign * self.count
        self.one = lax.ppermute(after(self.one, *others), "fsdp", self.ahead)
        both = self.count <= (n - 1) // 2
        if both:
            self.two = lax.ppermute(after(self.two, *others), "fsdp", self.back)
        self.target = self.store(self.target, ring_owner(self.place + hops, n), self.one)
        if both:
            self.target = self.store(self.target, ring_owner(self.place - hops, n), self.two)

    def rest(self):
        while self.count < self.n // 2:
            self.step()
        return self.target


class Scatter:
    def __init__(self, pick, n, flip):
        self.ahead, self.back = ring_pairs(n)
        self.sign = 1
        if flip:
            self.ahead, self.back, self.sign = self.back, self.ahead, -1
        self.place = ring_place(lax.axis_index("fsdp"), n)
        self.n, self.pick, self.count = n, pick, 0
        self.one = self.at(self.sign * (n // 2))
        self.two = self.at(-self.sign * ((n - 1) // 2))

    def at(self, offset, *blocks):
        return self.pick(ring_owner(self.place + offset, self.n), *blocks)

    def step(self, *others):
        if self.count == self.n // 2:
            return
        self.count += 1
        self.one = lax.ppermute(after(self.one, *others), "fsdp", self.ahead)
        both = self.count <= (self.n - 1) // 2
        if both:
            self.two = lax.ppermute(after(self.two, *others), "fsdp", self.back)
        left = self.n // 2 - self.count
        if left > 0:
            self.one = self.at(self.sign * left, self.one)
        left = (self.n - 1) // 2 - self.count
        if both and left > 0:
            self.two = self.at(-self.sign * left, self.two)

    def rest(self):
        while self.count < self.n // 2:
            self.step()
        return self.at(0, self.one, self.two)


def rows_of(array, size):
    def pick(owner, *blocks):
        value = lax.dynamic_slice_in_dim(array, owner * size, size, 0)
        if not blocks:
            return value
        value = value.astype(F32)
        for block in blocks:
            value = value + block.astype(F32)
        return value.astype(BF)

    return pick


def up_pick(up_g, attn_half, sums, shard):
    wide, narrow = up_g.shape[1], attn_half.shape[1]

    def pick(owner, *blocks):
        def body(owner_ref, up_ref, attn_ref, sums_ref, *refs):
            out_ref = refs[-1]

            def put(rows, cols, value):
                if blocks:
                    value = value.astype(F32)
                    for ref in refs[:-1]:
                        value = value + ref[rows, cols].astype(F32)
                out_ref[rows, cols] = value.astype(BF)

            top, below = slice(0, shard), slice(shard, shard + EXTRA)
            put(top, slice(0, wide), up_ref[...])
            put(top, slice(wide, wide + narrow), attn_ref[...])
            put(below, slice(0, sums.shape[1]), sums_ref[...])
            out_ref[below, sums.shape[1] :] = jnp.zeros(
                (EXTRA, wide + narrow - sums.shape[1]), BF
            )

        whole = pl.BlockSpec((shard + EXTRA, wide + narrow), lambda i, o: (0, 0))
        return pl.pallas_call(
            body,
            grid_spec=pltpu.PrefetchScalarGridSpec(
                num_scalar_prefetch=1,
                grid=(1,),
                in_specs=[
                    pl.BlockSpec((shard, wide), lambda i, o: (o[0], 0)),
                    pl.BlockSpec((shard, narrow), lambda i, o: (o[0], 0)),
                    pl.BlockSpec(sums.shape, lambda i, o: (0, 0)),
                ]
                + [whole] * len(blocks),
                out_specs=whole,
            ),
            out_shape=jax.ShapeDtypeStruct((shard + EXTRA, wide + narrow), BF),
            compiler_params=pltpu.CompilerParams(vmem_limit_bytes=16 << 20),
            cost_estimate=pl.CostEstimate(
                flops=1 << 20, bytes_accessed=(2 + len(blocks)) << 20, transcendentals=0
            ),
            name="up_pick",
        )(owner[None], up_g, attn_half, sums, *blocks)

    return pick


def normalize(values):
    average = jnp.mean(values, axis=-1, keepdims=True)
    centered = values - average
    variance = jnp.mean(centered * centered, axis=-1, keepdims=True)
    scale = lax.rsqrt(variance + EPS)
    return centered * scale, scale


def norm_back(unit, scale, gain, incoming):
    weighted = incoming * gain
    return (
        weighted
        - jnp.mean(weighted, axis=-1, keepdims=True)
        - unit * jnp.mean(weighted * unit, axis=-1, keepdims=True)
    ) * scale


def turned(value, cosine, sine_signed, inverse):
    width = value.shape[1]
    lane = lax.broadcasted_iota(jnp.int32, value.shape, 1)
    half = HEAD_DIM // 2
    other = jnp.where(
        lax.rem(lane, HEAD_DIM) < half,
        pltpu.roll(value, width - half, 1),
        pltpu.roll(value, half, 1),
    )
    repeat = width // cosine.shape[1]
    cosine = jnp.concatenate([cosine] * repeat, axis=1)
    sine_signed = jnp.concatenate([sine_signed] * repeat, axis=1)
    if inverse:
        return value * cosine - other * sine_signed
    return value * cosine + other * sine_signed


def project(hidden, weight, gain, cosine, sine_signed):
    rows, dim = hidden.shape
    width = weight.shape[1]
    pairs = width // (3 * PAIR)
    step = 512

    def body(hidden_ref, weight_ref, gain_ref, cos_ref, sin_ref, normed_ref, *out_refs):
        unit, _ = normalize(hidden_ref[...].astype(F32))
        normed = (unit * gain_ref[0:1, :].astype(F32)).astype(BF)
        normed_ref[...] = normed
        mixed = mm(normed, weight_ref[...])
        cos_part, sin_part = cos_ref[...], sin_ref[...]
        for p, out_ref in enumerate(out_refs):
            at = 3 * PAIR * p
            queries = turned(mixed[:, at : at + PAIR], cos_part, sin_part, False)
            out_ref[:, :PAIR] = (queries * (0.125 * math.log2(math.e))).astype(BF)
            out_ref[:, PAIR : 2 * PAIR] = turned(
                mixed[:, at + PAIR : at + 2 * PAIR], cos_part, sin_part, False
            ).astype(BF)
            out_ref[:, 2 * PAIR :] = mixed[:, at + 2 * PAIR : at + 3 * PAIR].astype(BF)

    return pl.pallas_call(
        body,
        grid=(rows // step,),
        in_specs=[
            pl.BlockSpec((step, dim), lambda i: (i, 0)),
            pl.BlockSpec((dim, width), lambda i: (0, 0)),
            pl.BlockSpec((EXTRA, dim), lambda i: (0, 0)),
            pl.BlockSpec((step, 128), lambda i: (i, 0)),
            pl.BlockSpec((step, 128), lambda i: (i, 0)),
        ],
        out_specs=[
            pl.BlockSpec((step, dim), lambda i: (i, 0)),
        ]
        + [pl.BlockSpec((step, 3 * PAIR), lambda i: (i, 0))] * pairs,
        out_shape=[jax.ShapeDtypeStruct((rows, dim), BF)]
        + [jax.ShapeDtypeStruct((rows, 3 * PAIR), BF)] * pairs,
        compiler_params=pltpu.CompilerParams(vmem_limit_bytes=32 << 20),
        cost_estimate=pl.CostEstimate(
            flops=2 * rows * dim * width, bytes_accessed=12 << 20, transcendentals=rows
        ),
        name="project",
    )(hidden, weight, gain, cosine, sine_signed)


def folded(value, op):
    rows, cols = value.shape
    return op(value.reshape(rows // 8, 8, cols), axis=0)


def head_columns(target, p, value_t, heads):
    for h in range(heads):
        at = slice(h * HEAD_DIM, (h + 1) * HEAD_DIM)
        if h:
            target[p, h, : h * HEAD_DIM, :] = jnp.zeros((h * HEAD_DIM, value_t.shape[1]), BF)
        target[p, h, at, :] = value_t[at, :]
        rest = (heads - 1 - h) * HEAD_DIM
        if rest:
            target[p, h, (h + 1) * HEAD_DIM :, :] = jnp.zeros((rest, value_t.shape[1]), BF)


def tile_mask(i, j, live, blk):
    key = j * blk + lax.broadcasted_iota(jnp.int32, (blk, blk), 0)
    query = i * blk + lax.broadcasted_iota(jnp.int32, (blk, blk), 1)
    return (key <= query) & (key < live)


def open_tiles(edge, nb):
    return sum(jnp.minimum(i, edge) for i in range(nb))


def next_open(i, j, edge, nb):
    end = j + 1 >= jnp.minimum(i, edge)
    return jnp.minimum(jnp.where(end, i + 1, i), nb - 1), jnp.where(end, 0, j + 1)


def attention(order, length, qkv, blk):
    rows = qkv.shape[0]
    width = qkv.shape[1] // 3
    heads = width // HEAD_DIM
    nb = rows // blk

    def body(order_ref, length_ref, qkv_ref, out_ref, lse_ref, keys, values_t, q_cols, even, odd, even_top, odd_top, total, tops, sums):
        live = length_ref[0]
        edge = lax.div(live, blk)

        def fill(p, carry):
            rows_at = pl.ds(pl.multiple_of(order_ref[p] * blk, blk), blk)
            keys[p] = qkv_ref[rows_at, width : 2 * width]
            values_t[p] = jnp.transpose(qkv_ref[rows_at, 2 * width :])
            head_columns(q_cols, p, jnp.transpose(qkv_ref[rows_at, :width]), heads)
            return carry

        lax.fori_loop(0, nb, fill, 0)

        def ahead(i, j, into, top, masks):
            key_block = keys[j]
            for h in range(heads):
                s = mm(key_block, q_cols[i, h])
                if masks:
                    s = jnp.where(tile_mask(i, j, live, blk), s, NEG)
                into[h] = s
                top[h] = folded(s, jnp.max)

        def work(i, j, scores, top, first):
            for h in range(heads):
                new = jnp.broadcast_to(jnp.max(top[h], axis=0, keepdims=True), (8, blk))
                if not first:
                    old = tops[i, h]
                    new = jnp.maximum(old, new)
                    shrink = jnp.exp2(old - new)
                tops[i, h] = new
                p = jnp.exp2(scores[h] - new[0:1])
                added = folded(p, jnp.sum)
                sums[i, h] = added if first else sums[i, h] * shrink + added
                at = slice(h * HEAD_DIM, (h + 1) * HEAD_DIM)
                product = mm(values_t[j, at, :], p.astype(BF))
                total[i, at, :] = product if first else total[i, at, :] * shrink[0:1] + product

        ahead(0, 0, even, even_top, True)

        def masked_pair(t, carry):
            i0 = 2 * t
            i1 = i0 + 1
            i2 = jnp.minimum(i0 + 2, nb - 1)
            ahead(i1, jnp.minimum(i1, edge), odd, odd_top, True)
            work(i0, jnp.minimum(i0, edge), even, even_top, True)
            ahead(i2, jnp.minimum(i2, edge), even, even_top, True)
            work(i1, jnp.minimum(i1, edge), odd, odd_top, True)
            return carry

        lax.fori_loop(0, nb // 2, masked_pair, 0)

        ahead(1, 0, even, even_top, False)

        def pair(t, place):
            i0, j0 = place
            i1, j1 = next_open(i0, j0, edge, nb)
            ahead(i1, j1, odd, odd_top, False)
            work(i0, j0, even, even_top, False)
            i2, j2 = next_open(i1, j1, edge, nb)
            ahead(i2, j2, even, even_top, False)
            work(i1, j1, odd, odd_top, False)
            return (i2, j2)

        count = open_tiles(edge, nb)
        i_last, j_last = lax.fori_loop(0, lax.div(count, 2), pair, (jnp.int32(1), jnp.int32(0)))

        @pl.when(lax.rem(count, 2) == 1)
        def _():
            work(i_last, j_last, even, even_top, False)

        def drain(p, carry):
            rows_at = pl.ds(pl.multiple_of(order_ref[p] * blk, blk), blk)
            scaled = []
            for h in range(heads):
                sum_h = jnp.sum(sums[p, h], axis=0, keepdims=True)
                lse_ref[p, h : h + 1, :] = tops[p, h][0:1] + jnp.log2(sum_h)
                scaled.append((total[p, h * HEAD_DIM : (h + 1) * HEAD_DIM, :] * (1.0 / sum_h)).astype(BF))
            out_ref[rows_at, :] = jnp.transpose(jnp.concatenate(scaled, axis=0))
            return carry

        lax.fori_loop(0, nb, drain, 0)

    vm = pl.BlockSpec(memory_space=pltpu.VMEM)
    sm = pl.BlockSpec(memory_space=pltpu.SMEM)
    return pl.pallas_call(
        body,
        in_specs=[sm, sm, vm],
        out_specs=[vm, vm],
        out_shape=[jax.ShapeDtypeStruct((rows, width), BF), jax.ShapeDtypeStruct((nb, 8, blk), F32)],
        scratch_shapes=[
            pltpu.VMEM((nb, blk, width), BF),
            pltpu.VMEM((nb, width, blk), BF),
            pltpu.VMEM((nb, heads, width, blk), BF),
            pltpu.VMEM((heads, blk, blk), F32),
            pltpu.VMEM((heads, blk, blk), F32),
            pltpu.VMEM((heads, 8, blk), F32),
            pltpu.VMEM((heads, 8, blk), F32),
            pltpu.VMEM((nb, width, blk), F32),
            pltpu.VMEM((nb, heads, 8, blk), F32),
            pltpu.VMEM((nb, heads, 8, blk), F32),
        ],
        compiler_params=pltpu.CompilerParams(vmem_limit_bytes=24 << 20),
        cost_estimate=pl.CostEstimate(
            flops=heads * 4500000000, bytes_accessed=3 << 20, transcendentals=heads << 21
        ),
        name="attention",
    )(order, length, qkv)


def attention_back(order, length, qkv, grad_out, out, lse, cosine, sine_signed, blk):
    rows = qkv.shape[0]
    width = qkv.shape[1] // 3
    heads = width // HEAD_DIM
    nb = rows // blk

    def body(
        order_ref, length_ref, qkv_ref, gout_ref, att_ref, lse_ref, cos_ref, sin_ref, result_ref,
        keys, keys_t, values, q_cols, q_rows, g_cols, g_rows, grad_q, grad_k, grad_v, inner,
        even_p, even_d, odd_p, odd_d,
    ):
        live = length_ref[0]
        edge = lax.div(live, blk)
        lane_head = lax.div(lax.broadcasted_iota(jnp.int32, (1, width), 1), HEAD_DIM)
        picks = [jnp.where(lane_head == h, 1.0, 0.0).astype(BF) for h in range(heads)]

        def fill(p, carry):
            rows_at = pl.ds(pl.multiple_of(order_ref[p] * blk, blk), blk)
            key_block = qkv_ref[rows_at, width : 2 * width]
            keys[p] = key_block
            keys_t[p] = jnp.transpose(key_block)
            values[p] = qkv_ref[rows_at, 2 * width :]
            grad_k[p] = jnp.zeros((blk, width), F32)
            grad_v[p] = jnp.zeros((blk, width), F32)
            query = qkv_ref[rows_at, :width]
            gout = gout_ref[rows_at, :]
            inner_t = jnp.transpose(gout.astype(F32) * att_ref[rows_at, :].astype(F32))
            head_columns(q_cols, p, jnp.transpose(query), heads)
            head_columns(g_cols, p, jnp.transpose(gout), heads)
            for h in range(heads):
                at = slice(h * blk, (h + 1) * blk)
                q_rows[p, at, :] = query * picks[h]
                g_rows[p, at, :] = gout * picks[h]
                inner[p, h : h + 1, :] = jnp.sum(
                    inner_t[h * HEAD_DIM : (h + 1) * HEAD_DIM, :], axis=0, keepdims=True
                )
            return carry

        lax.fori_loop(0, nb, fill, 0)

        def make(i, j, to_p, to_d, masks):
            key_block, value_block = keys[j], values[j]
            for h in range(heads):
                s = mm(key_block, q_cols[i, h])
                if masks:
                    s = jnp.where(tile_mask(i, j, live, blk), s, NEG)
                p = jnp.exp2(s - lse_ref[i, h : h + 1, :])
                d = p * (mm(value_block, g_cols[i, h]) - inner[i, h : h + 1, :])
                to_p[:, h * blk : (h + 1) * blk] = p.astype(BF)
                to_d[:, h * blk : (h + 1) * blk] = d.astype(BF)

        def use(i, j, from_p, from_d, first):
            grad_v[j] += mm(from_p[...], g_rows[i])
            grad_k[j] += mm(from_d[...], q_rows[i])
            for h in range(heads):
                at = slice(h * HEAD_DIM, (h + 1) * HEAD_DIM)
                product = mm(keys_t[j, at, :], from_d[:, h * blk : (h + 1) * blk])
                if first:
                    grad_q[i, at, :] = product
                else:
                    grad_q[i, at, :] += product

        make(0, 0, even_p, even_d, True)

        def masked_pair(t, carry):
            i0 = 2 * t
            i1 = i0 + 1
            i2 = jnp.minimum(i0 + 2, nb - 1)
            make(i1, jnp.minimum(i1, edge), odd_p, odd_d, True)
            use(i0, jnp.minimum(i0, edge), even_p, even_d, True)
            make(i2, jnp.minimum(i2, edge), even_p, even_d, True)
            use(i1, jnp.minimum(i1, edge), odd_p, odd_d, True)
            return carry

        lax.fori_loop(0, nb // 2, masked_pair, 0)

        make(1, 0, even_p, even_d, False)

        def pair(t, place):
            i0, j0 = place
            i1, j1 = next_open(i0, j0, edge, nb)
            make(i1, j1, odd_p, odd_d, False)
            use(i0, j0, even_p, even_d, False)
            i2, j2 = next_open(i1, j1, edge, nb)
            make(i2, j2, even_p, even_d, False)
            use(i1, j1, odd_p, odd_d, False)
            return (i2, j2)

        count = open_tiles(edge, nb)
        i_last, j_last = lax.fori_loop(0, lax.div(count, 2), pair, (jnp.int32(1), jnp.int32(0)))

        @pl.when(lax.rem(count, 2) == 1)
        def _():
            use(i_last, j_last, even_p, even_d, False)

        def drain(p, carry):
            rows_at = pl.ds(pl.multiple_of(order_ref[p] * blk, blk), blk)
            cos_part, sin_part = cos_ref[rows_at, :], sin_ref[rows_at, :]
            result_ref[rows_at, :width] = turned(jnp.transpose(grad_q[p]) * 0.125, cos_part, sin_part, True).astype(BF)
            result_ref[rows_at, width : 2 * width] = turned(grad_k[p] * math.log(2.0), cos_part, sin_part, True).astype(BF)
            result_ref[rows_at, 2 * width :] = grad_v[p].astype(BF)
            return carry

        lax.fori_loop(0, nb, drain, 0)

    vm = pl.BlockSpec(memory_space=pltpu.VMEM)
    sm = pl.BlockSpec(memory_space=pltpu.SMEM)
    return pl.pallas_call(
        body,
        in_specs=[sm, sm] + [vm] * 6,
        out_specs=vm,
        out_shape=jax.ShapeDtypeStruct((rows, 3 * width), BF),
        scratch_shapes=[
            pltpu.VMEM((nb, blk, width), BF),
            pltpu.VMEM((nb, width, blk), BF),
            pltpu.VMEM((nb, blk, width), BF),
            pltpu.VMEM((nb, heads, width, blk), BF),
            pltpu.VMEM((nb, heads * blk, width), BF),
            pltpu.VMEM((nb, heads, width, blk), BF),
            pltpu.VMEM((nb, heads * blk, width), BF),
            pltpu.VMEM((nb, width, blk), F32),
            pltpu.VMEM((nb, blk, width), F32),
            pltpu.VMEM((nb, blk, width), F32),
            pltpu.VMEM((nb, 8, blk), F32),
            pltpu.VMEM((blk, heads * blk), BF),
            pltpu.VMEM((blk, heads * blk), BF),
            pltpu.VMEM((blk, heads * blk), BF),
            pltpu.VMEM((blk, heads * blk), BF),
        ],
        compiler_params=pltpu.CompilerParams(vmem_limit_bytes=36 << 20),
        cost_estimate=pl.CostEstimate(
            flops=heads * 9000000000, bytes_accessed=6 << 20, transcendentals=heads << 21
        ),
        name="attention_back",
    )(order, length, qkv, grad_out, out, lse, cosine, sine_signed)


def gelu_both(u):
    scale = math.sqrt(2.0 / math.pi)
    inside = jnp.tanh(scale * (u + 0.044715 * u * u * u))
    value = 0.5 * u * (1.0 + inside)
    slope = 0.5 * (1.0 + inside) + 0.5 * u * (1.0 - inside * inside) * scale * (
        1.0 + 3.0 * 0.044715 * u * u
    )
    return value, slope


def bundle_up(q, w_qkv, w_attn, gain_rows, part):
    shard, dim = w_attn.shape
    pairs = part // PAIR

    def body(q_ref, qkv_ref, attn_ref, gain_ref, out_ref):
        at = q_ref[0] * part
        for p in range(pairs):
            for t in range(3):
                to = (3 * p + t) * PAIR
                out_ref[:shard, to : to + PAIR] = qkv_ref[
                    :, pl.ds(pl.multiple_of(t * dim + at + p * PAIR, PAIR), PAIR)
                ]
        out_ref[:shard, 3 * part :] = attn_ref[:, pl.ds(pl.multiple_of(at, part), part)]
        out_ref[shard:, :] = jnp.zeros((EXTRA, dim), BF)
        out_ref[shard:, : gain_ref.shape[1]] = gain_ref[...]

    return pl.pallas_call(
        body,
        in_specs=[SM, VM, VM, VM],
        out_specs=VM,
        out_shape=jax.ShapeDtypeStruct((shard + EXTRA, dim), BF),
        compiler_params=pltpu.CompilerParams(vmem_limit_bytes=8 << 20),
        name="bundle_up",
    )(q[None], w_qkv, w_attn, gain_rows)


def attention_end(q, came, attn_w, hidden, gains, blk):
    rows, dim = hidden.shape
    pairs = len(came)
    part = pairs * PAIR

    def body(q_ref, *refs):
        came_refs = refs[:pairs]
        weight_ref, hidden_ref, gain_ref, att_ref, branch_ref, middle_ref, normed_ref = refs[pairs:]
        for b in range(4):
            for p in range(pairs):
                at = b * part + p * PAIR
                att_ref[:, at : at + PAIR] = came_refs[p][lax.bitwise_xor(q_ref[0], b)]
        branch = mm(att_ref[...], weight_ref[...])
        branch_ref[...] = branch
        middle = hidden_ref[...].astype(F32) + normalize(branch)[0] * gain_ref[1:2, :].astype(F32)
        middle_ref[...] = middle
        normed_ref[...] = (normalize(middle)[0] * gain_ref[2:3, :].astype(F32)).astype(BF)

    row = pl.BlockSpec((blk, dim), lambda i: (i, 0))
    return pl.pallas_call(
        body,
        grid=(rows // blk,),
        in_specs=[SM]
        + [pl.BlockSpec((4, blk, PAIR), lambda i: (0, i, 0))] * pairs
        + [
            pl.BlockSpec(attn_w.shape, lambda i: (0, 0)),
            row,
            pl.BlockSpec(gains.shape, lambda i: (0, 0)),
        ],
        out_specs=[row] * 4,
        out_shape=[
            jax.ShapeDtypeStruct((rows, dim), BF),
            jax.ShapeDtypeStruct((rows, dim), F32),
            jax.ShapeDtypeStruct((rows, dim), F32),
            jax.ShapeDtypeStruct((rows, dim), BF),
        ],
        compiler_params=pltpu.CompilerParams(vmem_limit_bytes=24 << 20),
        cost_estimate=pl.CostEstimate(
            flops=2 * rows * dim * dim, bytes_accessed=10 << 20, transcendentals=0
        ),
        name="attention_end",
    )(q[None], *came, attn_w, hidden, gains)


def upstream_of(base_ref, length_ref, cotangent_ref, blk):
    pos = base_ref[pl.program_id(0)] * blk + lax.broadcasted_iota(jnp.int32, (blk, 1), 0)
    return cotangent_ref[...].astype(F32) * jnp.where(pos < length_ref[0], 1.0, 0.0)


def column_sums(value):
    return jnp.sum(value, axis=0, keepdims=True)


def top(bases, length, own, came, middle, cotangent, gains, blk):
    rows, dim = middle.shape

    def body(base_ref, length_ref, own_ref, came_ref, middle_ref, cot_ref, gain_ref, result_ref, grad_ref, sum_ref):
        gain = gain_ref[3:4, :].astype(F32)
        unit, scale = normalize(own_ref[...] + came_ref[...])
        result_ref[...] = (middle_ref[...] + unit * gain).astype(BF)
        upstream = upstream_of(base_ref, length_ref, cot_ref, blk)
        grad_ref[...] = norm_back(unit, scale, gain, upstream).astype(BF)

        @pl.when(pl.program_id(0) == 0)
        def _():
            sum_ref[...] = jnp.zeros_like(sum_ref)

        sum_ref[0:1, :] += column_sums(upstream * unit)

    row = pl.BlockSpec((blk, dim), lambda i: (i, 0))
    return pl.pallas_call(
        body,
        grid=(rows // blk,),
        in_specs=[SM, SM, row, row, row, row, pl.BlockSpec(gains.shape, lambda i: (0, 0))],
        out_specs=[row, row, pl.BlockSpec((8, dim), lambda i: (0, 0))],
        out_shape=[
            jax.ShapeDtypeStruct((rows, dim), BF),
            jax.ShapeDtypeStruct((rows, dim), BF),
            jax.ShapeDtypeStruct((8, dim), F32),
        ],
        compiler_params=pltpu.CompilerParams(vmem_limit_bytes=24 << 20),
        cost_estimate=pl.CostEstimate(flops=20 << 20, bytes_accessed=9 << 20, transcendentals=0),
        name="top",
    )(bases, length, own, came, middle, cotangent, gains)


def middle_back(q, bases, length, own, came, middle, branch, cotangent, gains, attn_w, last_sum, blk):
    rows, dim = middle.shape
    part = dim // 4
    pairs = part // PAIR
    steps = rows // blk

    def body(
        q_ref, base_ref, length_ref, own_ref, came_ref, middle_ref, branch_ref, cot_ref, gain_ref, weight_ref,
        last_ref, middle_out, branch_out, pieces_out, sums_out, attended, sums,
    ):
        i = pl.program_id(0)
        incoming = own_ref[...] + came_ref[...]
        unit, scale = normalize(middle_ref[...])
        grad_middle = upstream_of(base_ref, length_ref, cot_ref, blk) + norm_back(
            unit, scale, gain_ref[2:3, :].astype(F32), incoming
        )
        middle_out[...] = grad_middle
        sum2 = column_sums(incoming * unit)
        unit, scale = normalize(branch_ref[...])
        sum1 = column_sums(grad_middle * unit)
        grad_branch = norm_back(unit, scale, gain_ref[1:2, :].astype(F32), grad_middle).astype(BF)
        branch_out[...] = grad_branch
        attended[...] = mm_nt(grad_branch, weight_ref[...]).astype(BF)
        for g in range(4):
            at = lax.bitwise_xor(q_ref[0], g) * part
            for p in range(pairs):
                pieces_out[p, g] = attended[:, pl.ds(pl.multiple_of(at + p * PAIR, PAIR), PAIR)]

        @pl.when(i == 0)
        def _():
            sums[...] = jnp.zeros_like(sums)

        sums[0:1, :] += sum1
        sums[1:2, :] += sum2

        @pl.when(i == steps - 1)
        def _():
            sums[2:3, :] = last_ref[0:1, :]
            sums_out[...] = sums[...].astype(BF)

    row = pl.BlockSpec((blk, dim), lambda i: (i, 0))

    def whole(array):
        return pl.BlockSpec(array.shape, lambda i: (0, 0))

    return pl.pallas_call(
        body,
        grid=(steps,),
        in_specs=[SM, SM, SM, row, row, row, row, row, whole(gains), whole(attn_w), whole(last_sum)],
        out_specs=[
            row,
            row,
            pl.BlockSpec((pairs, 4, blk, PAIR), lambda i: (0, 0, i, 0)),
            pl.BlockSpec((EXTRA, dim), lambda i: (0, 0)),
        ],
        out_shape=[
            jax.ShapeDtypeStruct((rows, dim), F32),
            jax.ShapeDtypeStruct((rows, dim), BF),
            jax.ShapeDtypeStruct((pairs, 4, rows, PAIR), BF),
            jax.ShapeDtypeStruct((EXTRA, dim), BF),
        ],
        scratch_shapes=[pltpu.VMEM((blk, dim), BF), pltpu.VMEM((EXTRA, dim), F32)],
        compiler_params=pltpu.CompilerParams(vmem_limit_bytes=32 << 20),
        cost_estimate=pl.CostEstimate(
            flops=2 * rows * dim * dim, bytes_accessed=16 << 20, transcendentals=0
        ),
        name="middle_back",
    )(q[None], bases, length, own, came, middle, branch, cotangent, gains, attn_w, last_sum)


def bottom(own, from_core, from_x, hidden, grad_middle, gains, blk):
    rows, dim = hidden.shape

    def body(own_ref, core_ref, x_ref, hidden_ref, middle_ref, gain_ref, out_ref):
        incoming = own_ref[...] + core_ref[...].astype(F32) + x_ref[...].astype(F32)
        unit, scale = normalize(hidden_ref[...].astype(F32))
        out_ref[...] = middle_ref[...] + norm_back(
            unit, scale, gain_ref[0:1, :].astype(F32), incoming
        )

    row = pl.BlockSpec((blk, dim), lambda i: (i, 0))
    return pl.pallas_call(
        body,
        grid=(rows // blk,),
        in_specs=[row] * 5 + [pl.BlockSpec(gains.shape, lambda i: (0, 0))],
        out_specs=row,
        out_shape=jax.ShapeDtypeStruct((rows, dim), F32),
        compiler_params=pltpu.CompilerParams(vmem_limit_bytes=24 << 20),
        cost_estimate=pl.CostEstimate(flops=20 << 20, bytes_accessed=9 << 20, transcendentals=0),
        name="bottom",
    )(own, from_core, from_x, hidden, grad_middle, gains)


def up_end(c, mine, peer, shard, n, ff_half):
    wide = n * ff_half
    narrow = mine.shape[1] - wide
    if ff_half % 128:
        first = jnp.where(c == 0, mine, peer)[:shard]
        second = jnp.where(c == 0, peer, mine)[:shard]
        blocks = [v[:, :wide].reshape(shard, n, ff_half) for v in (first, second)]
        return (
            jnp.stack(blocks, axis=2).reshape(shard, 2 * wide),
            jnp.concatenate([first[:, wide:], second[:, wide:]], axis=1),
        )

    def body(c_ref, mine_ref, peer_ref, up_ref, attn_ref):
        def put(first, second):
            for s in range(n):
                at = slice(s * ff_half, (s + 1) * ff_half)
                up_ref[:, 2 * s * ff_half : (2 * s + 1) * ff_half] = first[:shard, at]
                up_ref[:, (2 * s + 1) * ff_half : (2 * s + 2) * ff_half] = second[:shard, at]
            attn_ref[:, :narrow] = first[:shard, wide:]
            attn_ref[:, narrow:] = second[:shard, wide:]

        @pl.when(c_ref[0] == 0)
        def _():
            put(mine_ref, peer_ref)

        @pl.when(c_ref[0] == 1)
        def _():
            put(peer_ref, mine_ref)

    return pl.pallas_call(
        body,
        in_specs=[SM, VM, VM],
        out_specs=[VM, VM],
        out_shape=[
            jax.ShapeDtypeStruct((shard, 2 * wide), F32),
            jax.ShapeDtypeStruct((shard, 2 * narrow), F32),
        ],
        compiler_params=pltpu.CompilerParams(vmem_limit_bytes=16 << 20),
        cost_estimate=pl.CostEstimate(flops=1 << 20, bytes_accessed=6 << 20, transcendentals=0),
        name="up_end",
    )(c[None], mine, peer)


def qkv_end(q, quarters, w_qkv, own_gains, late, part):
    shard, wide = w_qkv.shape
    pairs = len(quarters)
    dim = wide // 3

    def body(q_ref, *refs):
        quarter_refs = refs[:pairs]
        weight_ref, gain_ref, late_ref, out_ref, gains_ref = refs[pairs:]
        total = jnp.zeros((shard, PAIR), F32)
        for b in range(4):
            for p in range(pairs):
                block = quarter_refs[p][lax.bitwise_xor(q_ref[0], b)].astype(F32)
                for t in range(3):
                    at = t * dim + b * part + p * PAIR
                    value = block[:, t * PAIR : (t + 1) * PAIR]
                    out_ref[:, at : at + PAIR] = value
                    total = total + value * weight_ref[:, at : at + PAIR].astype(F32)
        first = jnp.sum(total, axis=1, keepdims=True) / gain_ref[:, 0:1].astype(F32)
        lane = lax.broadcasted_iota(jnp.int32, (shard, 4), 1)
        gains_ref[...] = jnp.where(lane == 0, first, late_ref[...])

    return pl.pallas_call(
        body,
        in_specs=[SM] + [VM] * (pairs + 3),
        out_specs=[VM, VM],
        out_shape=[
            jax.ShapeDtypeStruct((shard, wide), F32),
            jax.ShapeDtypeStruct((shard, 4), F32),
        ],
        compiler_params=pltpu.CompilerParams(vmem_limit_bytes=16 << 20),
        cost_estimate=pl.CostEstimate(flops=1 << 20, bytes_accessed=4 << 20, transcendentals=0),
        name="qkv_end",
    )(q[None], *quarters, w_qkv, own_gains, late)


def per_device(n, hidden_in, cotangent, lengths, block_of, w_qkv, w_attn, w_up, w_down, norm_gains):
    own_rows, dim = hidden_in.shape[1:]
    rows = 4 * own_rows
    blk = own_rows // 2
    ff = w_up.shape[1]
    shard = dim // n
    ff_half = ff // n // 2
    part = dim // 4
    pairs = part // PAIR
    q = lax.axis_index("ctx")
    c = lax.rem(q, 2)

    gain_rows = jnp.pad(norm_gains.T, ((0, EXTRA - 4), (0, 0)))
    bundle = bundle_up(q, w_qkv, w_attn, gain_rows, part)

    def store_bundle(target, owner, block):
        to_qkv, to_attn, to_gains = target
        return (
            lax.dynamic_update_slice(to_qkv, block[:shard, : 3 * part], (owner * shard, 0)),
            lax.dynamic_update_slice(to_attn, block[:shard, 3 * part :], (owner * shard, 0)),
            lax.dynamic_update_slice(to_gains, block[shard:, :shard], (0, owner * shard)),
        )

    def store_rows(target, owner, block):
        return lax.dynamic_update_slice(target, block, (owner * block.shape[0], 0))

    lead = Gather(
        bundle,
        n,
        False,
        store_bundle,
        (blank((dim, 3 * part), BF), blank((dim, part), BF), blank((EXTRA, dim), BF)),
    )
    lead.step()
    hidden_b = hidden_in[0]
    hidden_x = swap(after(hidden_b, bundle), 2)
    hidden_c = swap(after(hidden_b, bundle), 1)
    hidden_d = swap(hidden_x, 1)
    qkv_w, attn_q, gains = lead.rest()
    up_own = lax.dynamic_index_in_dim(
        w_up.reshape(shard, n, 2, ff_half), c, 2, keepdims=False
    ).reshape(shard, n * ff_half)
    down_own = lax.dynamic_slice_in_dim(w_down, c * ff_half, ff_half, 0)
    up = Gather(after(up_own, lead.one), n, False, store_rows, blank((dim, n * ff_half), BF))
    down = Gather(after(down_own, lead.one), n, True, store_rows, blank((n * ff_half, dim), BF))
    up.step()
    down.step()

    groups = [lax.bitwise_xor(q, g) for g in range(4)]
    blocks = jnp.concatenate([lax.dynamic_slice_in_dim(block_of, g, 1, 0)[0] for g in groups])
    order = jnp.sum(
        jnp.where(
            blocks[None, :] == jnp.arange(8, dtype=jnp.int32)[:, None],
            jnp.arange(8, dtype=jnp.int32)[None, :],
            0,
        ),
        axis=1,
        dtype=jnp.int32,
    )
    bases = blocks[:2]
    offsets = jnp.arange(blk, dtype=jnp.int32)
    pos = (blocks[:, None] * blk + offsets[None, :]).reshape(-1)
    lane = jnp.arange(128, dtype=jnp.int32)
    half_dim = HEAD_DIM // 2
    inverse = jnp.exp((lane % half_dim).astype(F32) * (-2.0 * math.log(10000.0) / HEAD_DIM))
    angles = pos.astype(F32)[:, None] * inverse[None, :]
    cosine = jnp.cos(angles)
    sine_signed = jnp.sin(angles) * jnp.where(lane % HEAD_DIM < half_dim, -1.0, 1.0)[None, :]

    hidden_all = blank((rows, dim), BF)
    for g, block in enumerate((hidden_b, hidden_c, hidden_x, hidden_d)):
        hidden_all = lax.dynamic_update_slice(hidden_all, block, (g * own_rows, 0))
    normed, *qkv = project(hidden_all, qkv_w, gains, cosine, sine_signed)
    up.step(qkv[0])
    attn_x = swap(attn_q, 2)
    attn_pair = swap(jnp.stack([attn_q, attn_x]), 1)
    attn_parts = jnp.stack([attn_q, attn_pair[0], attn_x, attn_pair[1]])
    attn_w = jnp.concatenate(
        [
            lax.dynamic_index_in_dim(attn_parts, lax.bitwise_xor(q, b), 0, keepdims=False)
            for b in range(4)
        ],
        axis=1,
    )
    att, lse, came = [], [], []
    for p in range(pairs):
        att_p, lse_p = attention(order, lengths, qkv[p], blk)
        att.append(att_p)
        lse.append(lse_p)
        att_g = att_p.reshape(4, own_rows, PAIR)
        came.append(jnp.stack([att_g[0]] + [swap(att_g[g], g) for g in range(1, 4)]))
    down.step(*att)
    attended, branch, middle, normed_mid = attention_end(q, came, attn_w, hidden_b, gains, blk)
    normed_mid2 = jnp.concatenate([normed_mid, swap(normed_mid, 1)], axis=0)
    up_w, down_w = up.rest(), down.rest()
    lifted = mm(normed_mid2, up_w)
    activated, slope = [v.astype(BF) for v in gelu_both(lifted)]
    lowered_c = swap(mm(activated[own_rows:], down_w), 1)
    lowered = mm(activated[:own_rows], down_w)
    result, grad_lowered, last_sum = top(
        bases, lengths, lowered, lowered_c, middle, cotangent[0], gains, blk
    )

    grad_lowered2 = jnp.concatenate([grad_lowered, swap(grad_lowered, 1)], axis=0)
    down_g = mm_tn(activated, grad_lowered2).astype(BF)
    down_ring = Scatter(rows_of(down_g, ff_half), n, False)
    down_ring.step()
    grad_lifted = (
        mm_nt(after(grad_lowered2, down_g), down_w) * slope.astype(F32)
    ).astype(BF)
    normed_mid_c = swap(mm_nt(grad_lifted[own_rows:], up_w), 1)
    grad_normed_mid = mm_nt(grad_lifted[:own_rows], up_w)
    grad_middle, grad_branch, pieces, sums = middle_back(
        q, bases, lengths, grad_normed_mid, normed_mid_c, middle, branch, cotangent[0], gains, attn_w, last_sum, blk
    )
    grad_out = [
        jnp.concatenate([pieces[p, 0]] + [swap(pieces[p, g], g) for g in range(1, 4)], axis=0)
        for p in range(pairs)
    ]
    attn_g = mm_tn(attended, grad_branch).astype(BF)
    half_cols = dim // 2
    attn_half = lax.dynamic_slice_in_dim(attn_g, c * half_cols, half_cols, 1).astype(F32) + swap(
        lax.dynamic_slice_in_dim(attn_g, (1 - c) * half_cols, half_cols, 1), 1
    ).astype(F32)
    attn_half = attn_half.astype(BF)
    up_g = mm_tn(normed_mid2, after(grad_lifted, pieces)).astype(BF)
    up_ring = Scatter(up_pick(up_g, attn_half, sums, shard), n, True)
    up_ring.step()
    grad_out[0] = after(grad_out[0], up_g)
    grad_mixed, rings = [], []
    for p in range(pairs):
        mixed_p = attention_back(
            order, lengths, qkv[p], grad_out[p], att[p], lse[p], cosine, sine_signed, blk
        )
        down_ring.step(mixed_p)
        qkv_g = mm_tn(normed, mixed_p).astype(BF)
        rings.append(Scatter(rows_of(qkv_g, shard), n, p % 2 == 1))
        grad_mixed.append(mixed_p)

    def normed_back(g):
        at = slice(g * own_rows, (g + 1) * own_rows)
        wide = 3 * PAIR
        return sum(
            mm_nt(grad_mixed[p][at], qkv_w[:, p * wide : (p + 1) * wide]) for p in range(pairs)
        )

    for_x = (normed_back(2) + swap(normed_back(3).astype(BF), 1).astype(F32)).astype(BF)
    from_x = swap(for_x, 2)
    from_core = swap(normed_back(1).astype(BF), 1)
    input_grad = bottom(normed_back(0), from_core, from_x, hidden_b, grad_middle, gains, blk)

    def both_x(value):
        return value.astype(F32) + swap(value, 2).astype(F32)

    down_x = both_x(down_ring.rest())
    down_c = swap(down_x, 1)
    down_out = jnp.concatenate(
        [jnp.where(c == 0, down_x, down_c), jnp.where(c == 0, down_c, down_x)], axis=0
    )
    up_x = both_x(up_ring.rest())
    up_c = swap(up_x, 1)
    up_out, attn_out = up_end(c, up_x, up_c, shard, n, ff_half)
    me = lax.axis_index("fsdp")
    late = lax.dynamic_slice(up_x, (shard, me * shard), (4, shard)) + lax.dynamic_slice(
        up_c, (shard, me * shard), (4, shard)
    )
    late = jnp.roll(late, 1, axis=0).T
    quarters = []
    for p in range(pairs):
        last = rings[p].rest()
        last_x = swap(last, 2)
        last_pair = swap(jnp.stack([last, last_x]), 1)
        quarters.append(jnp.stack([last, last_pair[0], last_x, last_pair[1]]))
    qkv_out, gains_out = qkv_end(q, quarters, w_qkv, norm_gains, late, part)
    return (
        result[None],
        input_grad[None],
        qkv_out,
        attn_out,
        up_out,
        down_out,
        gains_out,
    )


def solution(mesh):
    n = mesh.shape["fsdp"]

    def step(*args):
        return per_device(n, *args)

    rows = P("fsdp", "ctx", None)
    weight = P("fsdp", None)
    return jax.shard_map(
        step,
        mesh=mesh,
        in_specs=(rows, rows, P("fsdp"), P()) + (weight,) * 5,
        out_specs=(rows, rows) + (weight,) * 5,
        check_vma=False,
    )
```

time: 488 us -> 488 us (level)
  waiting for transfers between devices: 165 us -> 211 us
  other arithmetic: 44.8 us -> 18.5 us
  local copies, waits for them, and re-layouts: 53.8 us -> 44.4 us
  matrix products: 60.3 us -> 51.7 us
    ppermute x24 -> x33, waiting for transfers between devices: 34.6 us -> 58.8 us  [swap(): return lax.ppermute(value, 'ctx', [(i, i ^ bit) for i in range(4)])]
    ppermute x42 -> x49, waiting for transfers between devices: 131 us -> 152 us  [the longest x28 126 us: step(): self.one = lax.ppermute(after(self.one, *others), 'fsdp', self.ahead)]
    pallas_call x1 -> x2, Pallas kernels: 56.4 us -> 36.3 us  [attention_back(): pl.pallas_call(body, in_specs=[sm, sm] + [vm] * 6, out_specs=vm, out_shap...]
    pallas_call x0 -> x21, Pallas kernels: none -> 19.8 us  [the longest x1 6.44 us: middle_back(): pl.pallas_call(body, grid=(steps,), in_specs=[SM, SM, SM, row, row, row,...]
    dynamic_update_slice x16, local copies, waits for them, and re-layouts: 19.9 us -> 1.78 us  [store_rows(): return lax.dynamic_update_slice(target, block, (owner * block.shape[0], 0))]
    reduce_sum x10 -> x0, other arithmetic: 12.1 us -> none  [the longest x3 4.35 us: normalize(): average = jnp.mean(values, axis=-1, keepdims=True)]
    dot_general x4 -> x3, matrix products: 21.1 us -> 10.5 us  [mm(): return jnp.dot(left, right, preferred_element_type=F32)]
    unnamed x120 -> x106, local copies, waits for them, and re-layouts: 4.38 us -> 13.7 us
  transfers between devices with their start and end apart: 66 -> 82, of which waited for: 29 -> 33; matrix products, arithmetic and copies ran while one was open for 24% -> 15% of each run, Pallas kernels for 19% -> 16%
where the time goes in v2:
time: 488 us; the launch traced here: 479 us
  waiting for transfers between devices  211 us (43%)
  Pallas kernels  85.4 us (18%)
  starting transfers between devices  63.8 us (13%)
  matrix products  51.7 us (11%)
  local copies, waits for them, and re-layouts  44.4 us (9%)
  other arithmetic  18.5 us (4%)
    ppermute x28, waiting for transfers between devices, step(): self.one = lax.ppermute(after(self.one, *others), 'fsdp', self.ahead)  126 us
    ppermute x33, waiting for transfers between devices, swap(): return lax.ppermute(value, 'ctx', [(i, i ^ bit) for i in range(4)])  58.8 us
    pallas_call x2, Pallas kernels, attention_back(): pl.pallas_call(body, in_specs=[sm, sm] + [vm] * 6, out_specs=vm, out_shap...  36.3 us
    ppermute x28, starting transfers between devices, step(): self.one = lax.ppermute(after(self.one, *others), 'fsdp', self.ahead)  30.2 us
    ppermute x21, waiting for transfers between devices, step(): self.two = lax.ppermute(after(self.two, *others), 'fsdp', self.back)  26.3 us
    dot_general x11, matrix products, mm_nt(): lax.dot_general(left, right, (((1,), (1,)), ((), ())), preferred_element_...  24 us
    pallas_call x2, Pallas kernels, attention(): pl.pallas_call(body, in_specs=[sm, sm, vm], out_specs=[vm, vm], out_shape...  22.4 us
    ppermute x21, starting transfers between devices, step(): self.two = lax.ppermute(after(self.two, *others), 'fsdp', self.back)  19.5 us
  transfers between devices with their start and end apart: 82, of which 33 were waited for; matrix products, arithmetic and copies ran while one was open for 15% of the time, Pallas kernels for 16%

profile of v2, /device:TPU:0, one launch (start us, length us, event | category | flops | bytes accessed | tf_op | source)
XLA Modules:
  0.0 478.6 jit_solution(12975140929765210127)
XLA Ops:
  13.8 5.6 %fusion.14 = (f32[2048,128]{1,0:T(8,128)}, f32[2048,128]{1,0:T(8,128)}) fusion(f32[128]{0:T(128)S(1)} %get-tuple-element.143, f32[128]{0:T(128)S(1)} %get-tuple-element.144, f32[2048]{0:T(1024)S(1)} %bitcast.109), kind=kLoop, calls=%fused_computation.34 | loop fusion | flops 524288 | bytes 2106368 | tf_op jit(solution)/shard_map/mul | solution.py:912
  56.3 19.9 %collective-permute-done.19 = bf16[128,2048]{1,0:T(8,128)(2,1)S(1)} collective-permute-done((bf16[128,2048]{1,0:T(8,128)(2,1)S(1)}, bf16[128,2048]{1,0:T(8,128)(2,1)S(1)}, u32[]{:S(2)}, u32[]{:S(2)}) %collective-permute-start.19) | collective-permute-done | bytes 524320 | tf_op jit(solution)/shard_map/ppermute | solution.py:81
  80.1 6.9 %project.1 = (bf16[2048,1024]{1,0:T(8,128)(2,1)S(1)}, bf16[2048,384]{1,0:T(8,128)(2,1)S(1)}, bf16[2048,384]{1,0:T(8,128)(2,1)S(1)}) custom-call(bf16[2048,1024]{1,0:T(8,128)(2,1)S(1)} %copy-done.10, bf16[1024,768]{1,0:T(8,128)(2,1)S(1)} %slice_dynamic-update-slice_fusion.weight_ref, ...), custom_call_target="tpu_custom_call" | custom-call | flops 3221225472 | bytes 12582912 | tf_op jit(solution)/shard_map/project/pallas_call | solution.py:245
  87.0 11.2 %attention.2 = (bf16[2048,128]{1,0:T(8,128)(2,1)S(1)}, f32[8,8,256]{2,1,0:T(8,128)S(1)}) custom-call(s32[8]{0:T(128)S(1)} %select_reduce_fusion.order_ref, s32[1]{0:T(128)S(6)} %copy.73.length_ref, bf16[2048,384]{1,0:T(8,128)(2,1)S(1)} %get-tuple-element.44.qkv_ref), custom_call_target="tpu_custom_call" | custom-call | flops 8999999488 | bytes 3145728 | tf_op jit(solution)/shard_map/attention/pallas_call | solution.py:390
  98.3 11.2 %attention.3 = (bf16[2048,128]{1,0:T(8,128)(2,1)S(1)}, f32[8,8,256]{2,1,0:T(8,128)S(1)}) custom-call(s32[8]{0:T(128)S(1)} %select_reduce_fusion.order_ref, s32[1]{0:T(128)S(6)} %copy.73.length_ref, bf16[2048,384]{1,0:T(8,128)(2,1)S(1)} %get-tuple-element.46.qkv_ref), custom_call_target="tpu_custom_call" | custom-call | flops 8999999488 | bytes 3145728 | tf_op jit(solution)/shard_map/attention/pallas_call | solution.py:390
  133.0 11.2 %collective-permute-done.21 = bf16[128,2048]{1,0:T(8,128)(2,1)S(1)} collective-permute-done((bf16[128,2048]{1,0:T(8,128)(2,1)S(1)}, bf16[128,2048]{1,0:T(8,128)(2,1)S(1)}, u32[]{:S(2)}, u32[]{:S(2)}) %collective-permute-start.21) | collective-permute-done | bytes 524320 | tf_op jit(solution)/shard_map/ppermute | solution.py:81
  154.3 11.5 %collective-permute-done.23 = bf16[128,2048]{1,0:T(8,128)(2,1)S(1)} collective-permute-done((bf16[128,2048]{1,0:T(8,128)(2,1)S(1)}, bf16[128,2048]{1,0:T(8,128)(2,1)S(1)}, u32[]{:S(2)}, u32[]{:S(2)}) %collective-permute-start.23) | collective-permute-done | bytes 524320 | tf_op jit(solution)/shard_map/ppermute | solution.py:81
  166.4 8.1 %collective-permute-done.32 = bf16[256,1024]{1,0:T(8,128)(2,1)S(1)} collective-permute-done((bf16[256,1024]{1,0:T(8,128)(2,1)S(1)}, bf16[256,1024]{1,0:T(8,128)(2,1)S(1)}, u32[]{:S(2)}, u32[]{:S(2)}) %collective-permute-start.32) | collective-permute-done | bytes 524320 | tf_op jit(solution)/shard_map/ppermute | solution.py:81
  179.2 5.8 %multiply_convert_fusion.1 = (bf16[1024,2048]{1,0:T(8,128)(2,1)S(1)}, f32[1024,2048]{1,0:T(8,128)S(1)}) fusion(bf16[1024,1024]{1,0:T(8,128)(2,1)S(1)} %constant_dynamic-update-slice_fusion.28, bf16[1024,2048]{1,0:T(8,128)(2,1)S(1)} %constant_dynamic-update-slice_fusion.8), kind=kOutput, calls=%fused_computation.9 | convolution fusion | flops 4313841664 | bytes 18874368 | tf_op jit(solution)/shard_map/dot_general | solution.py:22
  198.0 6.2 %convolution_convert_fusion.1 = bf16[2048,1024]{1,0:T(8,128)(2,1)} fusion(bf16[1024,2048]{1,0:T(8,128)(2,1)S(1)} %get-tuple-element.141, bf16[1024,1024]{1,0:T(8,128)(2,1)S(1)} %constant_dynamic-update-slice_fusion.30), kind=kOutput, calls=%fused_computation.11 | convolution fusion | flops 4297064448 | bytes 10485760 | tf_op jit(solution)/shard_map/dot_general | solution.py:26
  204.3 9.1 %multiply_convert_fusion = bf16[1024,2048]{1,0:T(8,128)(2,1)S(1)} fusion(bf16[1024,1024]{1,0:T(8,128)(2,1)S(1)} %constant_dynamic-update-slice_fusion.30, bf16[2048,1024]{1,0:T(8,128)(2,1)S(1)} %constant_dynamic-update-slice_fusion, f32[1024,2048]{1,0:T(8,128)S(1)} %get-tuple-element.142), kind=kOutput, calls=%fused_computation.8 | convolution fusion | flops 4339007488 | bytes 18874368 | tf_op jit(solution)/shard_map/dot_general | solution.py:30
  221.5 5.3 %fusion.8.own_ref = f32[512,1024]{1,0:T(8,128)S(1)} fusion(bf16[1024,2048]{1,0:T(8,128)(2,1)} %copy-done.40, bf16[1024,2048]{1,0:T(8,128)(2,1)} %copy-done.48), kind=kOutput, calls=%fused_computation.14 | convolution fusion | flops 2147483648 | bytes 8388608 | tf_op jit(solution)/shard_map/dot_general | solution.py:30
  226.9 6.8 %collective-permute-done.73 = bf16[256,1024]{1,0:T(8,128)(2,1)S(1)} collective-permute-done((bf16[256,1024]{1,0:T(8,128)(2,1)S(1)}, bf16[256,1024]{1,0:T(8,128)(2,1)S(1)}, u32[]{:S(2)}, u32[]{:S(2)}) %collective-permute-start.73) | collective-permute-done | bytes 524320 | tf_op jit(solution)/shard_map/ppermute | solution.py:113
  233.9 6.4 %middle_back.1 = (f32[512,1024]{1,0:T(8,128)S(1)}, bf16[512,1024]{1,0:T(8,128)(2,1)S(1)}, bf16[2,4,512,128]{3,2,1,0:T(8,128)(2,1)S(1)}, bf16[16,1024]{1,0:T(8,128)(2,1)S(1)}) custom-call(s32[1]{0:T(128)} %bitcast.q_ref, s32[2]{0:T(128)S(1)} %get-tuple-element.94.base_ref, s32[1]{0:T(128)S(6)} %copy.73.length_ref, f32[512,1024]{1,0:T(8,128)S(1)} %fusion.8.own_ref, ...), custom_call_target="tpu_custom_call" | custom-call | flops 1073741824 | bytes 16777216 | tf_op jit(solution)/shard_map/middle_back/pallas_call | solution.py:719
  253.0 18.0 %attention_back.3 = bf16[2048,384]{1,0:T(8,128)(2,1)S(1)} custom-call(s32[8]{0:T(128)S(1)} %select_reduce_fusion.order_ref, s32[1]{0:T(128)S(6)} %copy.73.length_ref, bf16[2048,384]{1,0:T(8,128)(2,1)S(1)} %copy-done.36, bf16[2048,128]{1,0:T(8,128)(2,1)S(1)} %pad_maximum_fusion.7.gout_ref, bf16[2048,128]{1,0:T(8,128)(2,1)S(1)} %copy-done.27, ...), custom_call_target="tpu_custom_call" | custom-call | flops 17999998976 | bytes 6291456 | tf_op jit(solution)/shard_map/attention_back/pallas_call | solution.py:522
  274.3 18.2 %attention_back.2 = bf16[2048,384]{1,0:T(8,128)(2,1)S(1)} custom-call(s32[8]{0:T(128)S(1)} %select_reduce_fusion.order_ref, s32[1]{0:T(128)S(6)} %copy.73.length_ref, bf16[2048,384]{1,0:T(8,128)(2,1)S(1)} %copy-done.34, bf16[2048,128]{1,0:T(8,128)(2,1)S(1)} %pad_maximum_fusion.6.gout_ref, bf16[2048,128]{1,0:T(8,128)(2,1)S(1)} %get-tuple-element.45.att_ref, ...), custom_call_target="tpu_custom_call" | custom-call | flops 17999998976 | bytes 6291456 | tf_op jit(solution)/shard_map/attention_back/pallas_call | solution.py:522
  312.8 8.6 %collective-permute-done.64.refs_0_ = bf16[144,2560]{1,0:T(8,128)(2,1)S(1)} collective-permute-done((bf16[144,2560]{1,0:T(8,128)(2,1)S(1)}, bf16[144,2560]{1,0:T(8,128)(2,1)S(1)}, u32[]{:S(2)}, u32[]{:S(2)}) %collective-permute-start.64) | collective-permute-done | bytes 737312 | tf_op jit(solution)/shard_map/ppermute | solution.py:113
  324.7 18.5 %collective-permute-done.55 = bf16[128,384]{1,0:T(8,128)(2,1)S(1)} collective-permute-done((bf16[128,384]{1,0:T(8,128)(2,1)S(1)}, bf16[128,384]{1,0:T(8,128)(2,1)S(1)}, u32[]{:S(2)}, u32[]{:S(2)}) %collective-permute-start.55) | collective-permute-done | bytes 98336 | tf_op jit(solution)/shard_map/ppermute | solution.py:113
  355.1 24.4 %collective-permute-done.50 = bf16[128,384]{1,0:T(8,128)(2,1)S(1)} collective-permute-done((bf16[128,384]{1,0:T(8,128)(2,1)S(1)}, bf16[128,384]{1,0:T(8,128)(2,1)S(1)}, u32[]{:S(2)}, u32[]{:S(2)}) %collective-permute-start.50) | collective-permute-done | bytes 98336 | tf_op jit(solution)/shard_map/ppermute | solution.py:116
  387.5 9.3 %collective-permute-done.76 = bf16[256,1024]{1,0:T(8,128)(2,1)S(1)} collective-permute-done((bf16[256,1024]{1,0:T(8,128)(2,1)S(1)}, bf16[256,1024]{1,0:T(8,128)(2,1)S(1)}, u32[]{:S(2)}, u32[]{:S(2)}) %collective-permute-start.76) | collective-permute-done | bytes 524320 | tf_op jit(solution)/shard_map/ppermute | solution.py:113
  400.7 11.9 %collective-permute-done.57 = bf16[128,384]{1,0:T(8,128)(2,1)S(1)} collective-permute-done((bf16[128,384]{1,0:T(8,128)(2,1)S(1)}, bf16[128,384]{1,0:T(8,128)(2,1)S(1)}, u32[]{:S(2)}, u32[]{:S(2)}) %collective-permute-start.57) | collective-permute-done | bytes 98336 | tf_op jit(solution)/shard_map/ppermute | solution.py:113
  419.1 10.5 %collective-permute-done.80 = bf16[256,1024]{1,0:T(8,128)(2,1)S(1)} collective-permute-done((bf16[256,1024]{1,0:T(8,128)(2,1)S(1)}, bf16[256,1024]{1,0:T(8,128)(2,1)S(1)}, u32[]{:S(2)}, u32[]{:S(2)}) %collective-permute-start.80) | collective-permute-done | bytes 524320 | tf_op jit(solution)/shard_map/ppermute | solution.py:34
  429.7 17.7 %collective-permute-done.71 = bf16[144,2560]{1,0:T(8,128)(2,1)S(1)} collective-permute-done((bf16[144,2560]{1,0:T(8,128)(2,1)S(1)}, bf16[144,2560]{1,0:T(8,128)(2,1)S(1)}, u32[]{:S(2)}, u32[]{:S(2)}) %collective-permute-start.71) | collective-permute-done | bytes 737312 | tf_op jit(solution)/shard_map/ppermute | solution.py:34
  453.4 11.9 %collective-permute-done.44.x_ref = bf16[512,1024]{1,0:T(8,128)(2,1)S(1)} collective-permute-done((bf16[512,1024]{1,0:T(8,128)(2,1)S(1)}, bf16[512,1024]{1,0:T(8,128)(2,1)S(1)}, u32[]{:S(2)}, u32[]{:S(2)}) %collective-permute-start.44) | collective-permute-done | bytes 1048608 | tf_op jit(solution)/shard_map/ppermute | solution.py:34
  (394 shorter events, 200.4 us)
Async XLA Ops:
  6.7 38.9 %collective-permute-start = (bf16[512,1024]{1,0:T(8,128)(2,1)}, bf16[512,1024]{1,0:T(8,128)(2,1)}, u32[]{:S(2)}, u32[]{:S(2)}) collective-permute-start(bf16[512,1024]{1,0:T(8,128)(2,1)} %bitcast.82), channel_id=1, source_target_pairs={{0,8},{8,0},{16,24},{24,16},{1,9},{9,1},{17,25},{25,17},{2,10},{10... | collective-permute-start | bytes 3145736 | tf_op jit(solution)/shard_map/ppermute | solution.py:34
  6.7 38.8 %collective-permute-start.1 = (bf16[512,1024]{1,0:T(8,128)(2,1)}, bf16[512,1024]{1,0:T(8,128)(2,1)}, u32[]{:S(2)}, u32[]{:S(2)}) collective-permute-start(bf16[512,1024]{1,0:T(8,128)(2,1)} %bitcast.83), channel_id=1, source_target_pairs={{0,16},{8,24},{16,0},{24,8},{1,17},{9,25},{17,1},{25,9},{2,18},{10... | collective-permute-start | bytes 3145736 | tf_op jit(solution)/shard_map/ppermute | solution.py:34
  45.5 31.3 %collective-permute-start.2 = (bf16[512,1024]{1,0:T(8,128)(2,1)}, bf16[512,1024]{1,0:T(8,128)(2,1)S(1)}, u32[]{:S(2)}, u32[]{:S(2)}) collective-permute-start(bf16[512,1024]{1,0:T(8,128)(2,1)} %collective-permute-done.1), channel_id=1, source_target_pairs={{0,8},{8,0},{16,24},{24,16},{1,9},{9,1},{17,25},{25,17},{2,10},{10... | collective-permute-start | bytes 3145736 | tf_op jit(solution)/shard_map/ppermute | solution.py:34
  50.4 59.3 %collective-permute-start.26 = (bf16[256,1024]{1,0:T(8,128)(2,1)}, bf16[256,1024]{1,0:T(8,128)(2,1)S(1)}, u32[]{:S(2)}, u32[]{:S(2)}) collective-permute-start(bf16[256,1024]{1,0:T(8,128)(2,1)} %constant_dynamic-slice_fusion.7), channel_id=1, source_target_pairs={{2,0},{4,2},{6,4},{7,6},{5,7},{3,5},{1,3},{0,1},{10,8},{12,10},{14... | collective-permute-start | bytes 1572872 | tf_op jit(solution)/shard_map/ppermute | solution.py:81
  51.1 60.1 %collective-permute-start.27 = (bf16[256,1024]{1,0:T(8,128)(2,1)}, bf16[256,1024]{1,0:T(8,128)(2,1)S(1)}, u32[]{:S(2)}, u32[]{:S(2)}) collective-permute-start(bf16[256,1024]{1,0:T(8,128)(2,1)} %constant_dynamic-slice_fusion.7), channel_id=1, source_target_pairs={{0,2},{2,4},{4,6},{6,7},{7,5},{5,3},{3,1},{1,0},{8,10},{10,12},{12... | collective-permute-start | bytes 1572872 | tf_op jit(solution)/shard_map/ppermute | solution.py:84
  54.0 58.8 %collective-permute-start.20 = (bf16[128,2048]{1,0:T(8,128)(2,1)S(1)}, bf16[128,2048]{1,0:T(8,128)(2,1)S(1)}, u32[]{:S(2)}, u32[]{:S(2)}) collective-permute-start(bf16[128,2048]{1,0:T(8,128)(2,1)S(1)} %bitcast.90), channel_id=1, source_target_pairs={{2,0},{4,2},{6,4},{7,6},{5,7},{3,5},{1,3},{0,1},{10,8},{12,10},{14... | collective-permute-start | bytes 1572872 | tf_op jit(solution)/shard_map/ppermute | solution.py:84
  76.2 35.5 %collective-permute-start.16 = (bf16[1024,256]{1,0:T(8,128)(2,1)}, bf16[1024,256]{1,0:T(8,128)(2,1)S(1)}, u32[]{:S(2)}, u32[]{:S(2)}) collective-permute-start(bf16[1024,256]{1,0:T(8,128)(2,1)} %slice_dynamic-update-slice_fusion.8), channel_id=1, source_target_pairs={{0,16},{8,24},{16,0},{24,8},{1,17},{9,25},{17,1},{25,9},{2,18},{10... | collective-permute-start | bytes 1572872 | tf_op jit(solution)/shard_map/ppermute | solution.py:34
  133.0 33.3 %collective-permute-start.31 = (bf16[256,1024]{1,0:T(8,128)(2,1)S(1)}, bf16[256,1024]{1,0:T(8,128)(2,1)S(1)}, u32[]{:S(2)}, u32[]{:S(2)}) collective-permute-start(bf16[256,1024]{1,0:T(8,128)(2,1)S(1)} %collective-permute-done.29), channel_id=1, source_target_pairs={{0,2},{2,4},{4,6},{6,7},{7,5},{5,3},{3,1},{1,0},{8,10},{10,12},{12... | collective-permute-start | bytes 1572872 | tf_op jit(solution)/shard_map/ppermute | solution.py:84
  220.1 124.2 %collective-permute-start.77 = (bf16[256,1024]{1,0:T(8,128)(2,1)}, bf16[256,1024]{1,0:T(8,128)(2,1)}, u32[]{:S(2)}, u32[]{:S(2)}) collective-permute-start(bf16[256,1024]{1,0:T(8,128)(2,1)} %get-tuple-element.102), channel_id=1, source_target_pairs={{2,0},{4,2},{6,4},{7,6},{5,7},{3,5},{1,3},{0,1},{10,8},{12,10},{14... | collective-permute-start | bytes 1572872 | tf_op jit(solution)/shard_map/ppermute | solution.py:116
  242.5 30.7 %collective-permute-start.38 = (bf16[512,128]{1,0:T(8,128)(2,1)S(1)}, bf16[512,128]{1,0:T(8,128)(2,1)}, u32[]{:S(2)}, u32[]{:S(2)}) collective-permute-start(bf16[512,128]{1,0:T(8,128)(2,1)S(1)} %get-tuple-element.114), channel_id=1, source_target_pairs={{0,24},{8,16},{16,8},{24,0},{1,25},{9,17},{17,9},{25,1},{2,26},{10... | collective-permute-start | bytes 393224 | tf_op jit(solution)/shard_map/ppermute | solution.py:34
  252.0 48.2 %collective-permute-start.63 = (bf16[1024,512]{1,0:T(8,128)(2,1)}, bf16[1024,512]{1,0:T(8,128)(2,1)}, u32[]{:S(2)}, u32[]{:S(2)}) collective-permute-start(bf16[1024,512]{1,0:T(8,128)(2,1)} %constant_dynamic-slice_fusion.2), channel_id=1, source_target_pairs={{0,8},{8,0},{16,24},{24,16},{1,9},{9,1},{17,25},{25,17},{2,10},{10... | collective-permute-start | bytes 3145736 | tf_op jit(solution)/shard_map/ppermute | solution.py:34
  311.2 34.2 %collective-permute-start.75 = (bf16[256,1024]{1,0:T(8,128)(2,1)S(1)}, bf16[256,1024]{1,0:T(8,128)(2,1)S(1)}, u32[]{:S(2)}, u32[]{:S(2)}) collective-permute-start(bf16[256,1024]{1,0:T(8,128)(2,1)S(1)} %add_convert_fusion.8), channel_id=1, source_target_pairs={{0,2},{2,4},{4,6},{6,7},{7,5},{5,3},{3,1},{1,0},{8,10},{10,12},{12... | collective-permute-start | bytes 1572872 | tf_op jit(solution)/shard_map/ppermute | solution.py:113
  349.0 32.2 %collective-permute-start.78 = (bf16[256,1024]{1,0:T(8,128)(2,1)S(1)}, bf16[256,1024]{1,0:T(8,128)(2,1)S(1)}, u32[]{:S(2)}, u32[]{:S(2)}) collective-permute-start(bf16[256,1024]{1,0:T(8,128)(2,1)S(1)} %get-tuple-element.76), channel_id=1, source_target_pairs={{2,0},{4,2},{6,4},{7,6},{5,7},{3,5},{1,3},{0,1},{10,8},{12,10},{14... | collective-permute-start | bytes 1572872 | tf_op jit(solution)/shard_map/ppermute | solution.py:116
  350.3 31.6 %collective-permute-start.69 = (bf16[144,2560]{1,0:T(8,128)(2,1)S(1)}, bf16[144,2560]{1,0:T(8,128)(2,1)S(1)}, u32[]{:S(2)}, u32[]{:S(2)}) collective-permute-start(bf16[144,2560]{1,0:T(8,128)(2,1)S(1)} %up_pick.13), channel_id=1, source_target_pairs={{0,2},{2,4},{4,6},{6,7},{7,5},{5,3},{3,1},{1,0},{8,10},{10,12},{12... | collective-permute-start | bytes 2211848 | tf_op jit(solution)/shard_map/ppermute | solution.py:116
  351.3 32.2 %collective-permute-start.66 = (bf16[144,2560]{1,0:T(8,128)(2,1)S(1)}, bf16[144,2560]{1,0:T(8,128)(2,1)S(1)}, u32[]{:S(2)}, u32[]{:S(2)}) collective-permute-start(bf16[144,2560]{1,0:T(8,128)(2,1)S(1)} %up_pick.10), channel_id=1, source_target_pairs={{2,0},{4,2},{6,4},{7,6},{5,7},{3,5},{1,3},{0,1},{10,8},{12,10},{14... | collective-permute-start | bytes 2211848 | tf_op jit(solution)/shard_map/ppermute | solution.py:113
  353.4 31.6 %collective-permute-start.48 = (bf16[128,384]{1,0:T(8,128)(2,1)S(1)}, bf16[128,384]{1,0:T(8,128)(2,1)S(1)}, u32[]{:S(2)}, u32[]{:S(2)}) collective-permute-start(bf16[128,384]{1,0:T(8,128)(2,1)S(1)} %get-tuple-element.123), channel_id=1, source_target_pairs={{0,2},{2,4},{4,6},{6,7},{7,5},{5,3},{3,1},{1,0},{8,10},{10,12},{12... | collective-permute-start | bytes 294920 | tf_op jit(solution)/shard_map/ppermute | solution.py:113
  385.1 33.3 %collective-permute-start.43 = (bf16[512,1024]{1,0:T(8,128)(2,1)S(1)}, bf16[512,1024]{1,0:T(8,128)(2,1)S(1)}, u32[]{:S(2)}, u32[]{:S(2)}) collective-permute-start(bf16[512,1024]{1,0:T(8,128)(2,1)S(1)} %add_convert_fusion.2), channel_id=1, source_target_pairs={{0,8},{8,0},{16,24},{24,16},{1,9},{9,1},{17,25},{25,17},{2,10},{10... | collective-permute-start | bytes 3145736 | tf_op jit(solution)/shard_map/ppermute | solution.py:34
  385.3 29.4 %collective-permute-start.70 = (bf16[144,2560]{1,0:T(8,128)(2,1)S(1)}, bf16[144,2560]{1,0:T(8,128)(2,1)S(1)}, u32[]{:S(2)}, u32[]{:S(2)}) collective-permute-start(bf16[144,2560]{1,0:T(8,128)(2,1)S(1)} %up_pick.14), channel_id=1, source_target_pairs={{0,2},{2,4},{4,6},{6,7},{7,5},{5,3},{3,1},{1,0},{8,10},{10,12},{12... | collective-permute-start | bytes 2211848 | tf_op jit(solution)/shard_map/ppermute | solution.py:116
  387.0 27.8 %collective-permute-start.67 = (bf16[144,2560]{1,0:T(8,128)(2,1)S(1)}, bf16[144,2560]{1,0:T(8,128)(2,1)S(1)}, u32[]{:S(2)}, u32[]{:S(2)}) collective-permute-start(bf16[144,2560]{1,0:T(8,128)(2,1)S(1)} %up_pick.11), channel_id=1, source_target_pairs={{2,0},{4,2},{6,4},{7,6},{5,7},{3,5},{1,3},{0,1},{10,8},{12,10},{14... | collective-permute-start | bytes 2211848 | tf_op jit(solution)/shard_map/ppermute | solution.py:113
  414.7 38.7 %collective-permute-start.42 = (bf16[512,1024]{1,0:T(8,128)(2,1)S(1)}, bf16[512,1024]{1,0:T(8,128)(2,1)S(1)}, u32[]{:S(2)}, u32[]{:S(2)}) collective-permute-start(bf16[512,1024]{1,0:T(8,128)(2,1)S(1)} %add_convert_fusion.3), channel_id=1, source_target_pairs={{0,8},{8,0},{16,24},{24,16},{1,9},{9,1},{17,25},{25,17},{2,10},{10... | collective-permute-start | bytes 3145736 | tf_op jit(solution)/shard_map/ppermute | solution.py:34
  414.8 32.9 %collective-permute-start.61 = (bf16[128,384]{1,0:T(8,128)(2,1)S(1)}, bf16[128,384]{1,0:T(8,128)(2,1)S(1)}, u32[]{:S(2)}, u32[]{:S(2)}) collective-permute-start(bf16[128,384]{1,0:T(8,128)(2,1)S(1)} %add_convert_fusion.10), channel_id=1, source_target_pairs={{0,16},{8,24},{16,0},{24,8},{1,17},{9,25},{17,1},{25,9},{2,18},{10... | collective-permute-start | bytes 294920 | tf_op jit(solution)/shard_map/ppermute | solution.py:34
  418.3 29.1 %collective-permute-start.71 = (bf16[144,2560]{1,0:T(8,128)(2,1)S(1)}, bf16[144,2560]{1,0:T(8,128)(2,1)S(1)}, u32[]{:S(2)}, u32[]{:S(2)}) collective-permute-start(bf16[144,2560]{1,0:T(8,128)(2,1)S(1)} %up_pick.15), channel_id=1, source_target_pairs={{0,16},{8,24},{16,0},{24,8},{1,17},{9,25},{17,1},{25,9},{2,18},{10... | collective-permute-start | bytes 2211848 | tf_op jit(solution)/shard_map/ppermute | solution.py:34
  418.4 30.7 %collective-permute-start.53 = (bf16[2,128,384]{2,1,0:T(8,128)(2,1)S(1)}, bf16[2,128,384]{2,1,0:T(8,128)(2,1)S(1)}, u32[]{:S(2)}, u32[]{:S(2)}) collective-permute-start(bf16[2,128,384]{2,1,0:T(8,128)(2,1)S(1)} %pad_maximum_fusion.10), channel_id=1, source_target_pairs={{0,8},{8,0},{16,24},{24,16},{1,9},{9,1},{17,25},{25,17},{2,10},{10... | collective-permute-start | bytes 589832 | tf_op jit(solution)/shard_map/ppermute | solution.py:34
  429.6 35.7 %collective-permute-start.44 = (bf16[512,1024]{1,0:T(8,128)(2,1)S(1)}, bf16[512,1024]{1,0:T(8,128)(2,1)S(1)}, u32[]{:S(2)}, u32[]{:S(2)}) collective-permute-start(bf16[512,1024]{1,0:T(8,128)(2,1)S(1)} %add_convert_fusion.1), channel_id=1, source_target_pairs={{0,16},{8,24},{16,0},{24,8},{1,17},{9,25},{17,1},{25,9},{2,18},{10... | collective-permute-start | bytes 3145736 | tf_op jit(solution)/shard_map/ppermute | solution.py:34
  (108 other events, 1258.2 us)
